TPU v7x, 32 devices: a whole 2x2x4 slice. The times are simulated.
32 devices in a mesh: dp: 8 (over z, x), tensor: 4 (over y, core).
Axes of the slice: x: 2, y: 2, z: 4, core: 2. Of those that a mesh axis runs over, the one named last changes fastest.
Arguments:
- hidden_in: bfloat16 [512, 16, 768], P('tensor', 'dp'), may hold values from -2.5 to 2.5
- cotangent: bfloat16 [512, 16, 768], P('tensor', 'dp'), may hold values from -2.5 to 2.5
- doc_lengths: int32 [16, 5], P('dp'), may hold values from 1 to 385, 512 in all within a row
- pad_count: int32 [16], P('dp'), may hold values from 1 to 32
- input_weight: bfloat16 [2, 3, 768, 768], P(None, None, None, 'tensor'), may hold values from -0.21875 to 0.21875
- input_bias: bfloat16 [2, 2, 768], P(None, None, 'tensor'), may hold values from -1.5 to 1.5
- output_weight: bfloat16 [2, 768, 768], P(None, 'tensor'), may hold values from -0.875 to 0.875
- up_weight: bfloat16 [2, 768, 3072], P(None, None, 'tensor'), may hold values from -0.21875 to 0.21875
- up_bias: bfloat16 [2, 3072], P(None, 'tensor'), may hold values from -1.5 to 1.5
- down_weight: bfloat16 [2, 3072, 768], P(None, 'tensor'), may hold values from -0.109375 to 0.109375
- branch_bias: bfloat16 [2, 2, 768], replicated, may hold values from -1.5 to 1.5
- norm_gain: bfloat16 [2, 2, 768], replicated, may hold values from 0.3984375 to 1.59375
- norm_shift: bfloat16 [2, 2, 768], replicated, may hold values from -1.5 to 1.5
Outputs:
- hidden_out: bfloat16 [512, 16, 768], P('tensor', 'dp')
- grad_hidden: float32 [512, 16, 768], P('tensor', 'dp')
- grad_input_weight: float32 [2, 3, 768, 768], P(None, None, None, 'tensor')
- grad_input_bias: float32 [2, 2, 768], P(None, None, 'tensor')
- grad_output_weight: float32 [2, 768, 768], P(None, 'tensor')
- grad_up_weight: float32 [2, 768, 3072], P(None, None, 'tensor')
- grad_up_bias: float32 [2, 3072], P(None, 'tensor')
- grad_down_weight: float32 [2, 3072, 768], P(None, 'tensor')
- grad_branch_bias: float32 [2, 2, 768], replicated
- grad_norm_gain: float32 [2, 2, 768], replicated
- grad_norm_shift: float32 [2, 2, 768], replicated
Inputs may be any that keep to these rules, and one draw needn't show every extreme that they name: `doc_lengths`: each row's 5 lengths add up to 512; in every row the longest text has exactly 385 positions.
All inputs are finite; a program needn't handle non-finite values.
Results may differ from a plain program's by a relative error of at most 0.029.
Values may be sent and summed in bfloat16 or wider, within the bound.
A program may use at most 128 MiB of HBM per device.

v0:
```python
import jax
import jax.numpy as jnp
from jax import lax
from jax.sharding import PartitionSpec as P

HEAD_DIM = 64


epsilon = 1e-05
masked_value = -1e30


def normalize(value, gain, shift):
    average = jnp.mean(value, axis=-1, keepdims=True)
    centered = value - average
    variance = jnp.mean(centered * centered, axis=-1, keepdims=True)
    return centered * lax.rsqrt(variance + epsilon) * gain + shift


def residual_norm(base, branch, bias, gain, shift):
    return normalize(base + branch + bias, gain, shift)


def gelu(value):
    return 0.5 * value * (1.0 + lax.erf(value * 0.7071067811865476))


def segment_table(lengths, padding, seq_len):
    ends = jnp.cumsum(lengths, axis=1)
    position = jnp.arange(seq_len, dtype=jnp.int32)
    index = jnp.sum((position[:, None, None] >= ends[None, :, :]).astype(jnp.int32), axis=2)
    padded = position[:, None] >= (seq_len - padding)[None, :]
    return jnp.where(padded, lengths.shape[1], index)


def split_heads(value):
    return value.reshape(value.shape[0], value.shape[1], -1, HEAD_DIM)


def join_heads(value):
    return value.reshape(value.shape[0], value.shape[1], -1)


def attend_forward(stacked, allowed):
    query, keys, values = (
        split_heads(stacked[0]),
        split_heads(stacked[1]),
        split_heads(stacked[2]),
    )
    scores = jnp.einsum(
        "qrhe,krhe->rhqk", query, keys, preferred_element_type=jnp.float32
    ) * HEAD_DIM ** (-0.5)
    masked = jnp.where(allowed, scores, masked_value)
    largest = jnp.max(masked, axis=-1, keepdims=True)
    powers = jnp.exp(masked - largest)
    total = jnp.sum(powers, axis=-1, keepdims=True)
    probs = powers / total
    context = jnp.einsum(
        "rhqk,krhe->qrhe", probs.astype(jnp.bfloat16), values, preferred_element_type=jnp.float32
    )
    return (join_heads(context).astype(jnp.bfloat16), largest + jnp.log(total))


def attend_backward(stacked, allowed, log_total, grad_context):
    scale = HEAD_DIM ** (-0.5)
    query, keys, values = (
        split_heads(stacked[0]),
        split_heads(stacked[1]),
        split_heads(stacked[2]),
    )
    upstream = split_heads(grad_context)
    scores = jnp.einsum("qrhe,krhe->rhqk", query, keys, preferred_element_type=jnp.float32) * scale
    probs = jnp.exp(jnp.where(allowed, scores, masked_value) - log_total)
    grad_probs = jnp.einsum("qrhe,krhe->rhqk", upstream, values, preferred_element_type=jnp.float32)
    grad_values = jnp.einsum(
        "rhqk,qrhe->krhe", probs.astype(jnp.bfloat16), upstream, preferred_element_type=jnp.float32
    )
    inner = jnp.sum(probs * grad_probs, axis=-1, keepdims=True)
    grad_scores = (probs * (grad_probs - inner)).astype(jnp.bfloat16)
    grad_query = (
        jnp.einsum("rhqk,krhe->qrhe", grad_scores, keys, preferred_element_type=jnp.float32) * scale
    )
    grad_keys = (
        jnp.einsum("rhqk,qrhe->krhe", grad_scores, query, preferred_element_type=jnp.float32)
        * scale
    )
    return jnp.stack(
        [join_heads(grad_query), join_heads(grad_keys), join_heads(grad_values)]
    ).astype(jnp.bfloat16)


def layer_forward(hidden, allowed, weights):
    in_weight, in_bias, out_weight, wide_weight, wide_bias, narrow_weight, biases, gains, shifts = (
        weights
    )
    projected = jnp.einsum(
        "srd,cde->csre",
        lax.all_gather(hidden.astype(jnp.bfloat16), "tensor", axis=0, tiled=True),
        in_weight,
        preferred_element_type=jnp.float32,
    )
    stacked = jnp.stack(
        [projected[0] + in_bias[0], projected[1], projected[2] + in_bias[1]]
    ).astype(jnp.bfloat16)
    context, log_total = attend_forward(stacked, allowed)
    part = context
    mixed = lax.psum_scatter(
        jnp.einsum("srd,de->sre", part, out_weight, preferred_element_type=jnp.float32),
        "tensor",
        scatter_dimension=0,
        tiled=True,
    )
    first = residual_norm(hidden, mixed, biases[0], gains[0], shifts[0])
    wide = (
        jnp.einsum(
            "srd,df->srf",
            lax.all_gather(first.astype(jnp.bfloat16), "tensor", axis=0, tiled=True),
            wide_weight,
            preferred_element_type=jnp.float32,
        )
        + wide_bias
    )
    activated = gelu(wide).astype(jnp.bfloat16)
    part = activated
    fed = lax.psum_scatter(
        jnp.einsum("srf,fd->srd", part, narrow_weight, preferred_element_type=jnp.float32).astype(
            jnp.bfloat16
        ),
        "tensor",
        scatter_dimension=0,
        tiled=True,
    ).astype(jnp.float32)
    result = residual_norm(first, fed, biases[1], gains[1], shifts[1])
    return (result, (hidden, stacked, context, log_total, mixed, first, wide, activated, fed))


def layer_backward(upstream, allowed, weights, cache):
    in_weight, in_bias, out_weight, wide_weight, wide_bias, narrow_weight, biases, gains, shifts = (
        weights
    )
    hidden, stacked, context, log_total, mixed, first, wide, activated, fed = cache
    unused, pull_second = jax.vjp(residual_norm, first, fed, biases[1], gains[1], shifts[1])
    grad_first, grad_fed, bias_two, gain_two, shift_two = pull_second(upstream)
    piece = lax.all_gather(grad_fed.astype(jnp.bfloat16), "tensor", axis=0, tiled=True)
    rows = activated
    weight_total = jnp.einsum("srf,srd->fd", rows, piece, preferred_element_type=jnp.float32)
    update = jnp.einsum("srd,fd->srf", piece, narrow_weight, preferred_element_type=jnp.float32)
    spread = update
    grad_narrow = weight_total
    grad_activated = spread
    unused, pull_gelu = jax.vjp(gelu, wide)
    grad_wide = pull_gelu(grad_activated)[0].astype(jnp.bfloat16)
    grad_wide_bias = jnp.sum(grad_wide, axis=(0, 1), dtype=jnp.float32)
    part = grad_wide
    grad_first = grad_first + lax.psum_scatter(
        jnp.einsum("srf,df->srd", part, wide_weight, preferred_element_type=jnp.float32).astype(
            jnp.bfloat16
        ),
        "tensor",
        scatter_dimension=0,
        tiled=True,
    ).astype(jnp.float32)
    rows = grad_wide
    grad_wide_weight = jnp.einsum(
        "srd,srf->df",
        lax.all_gather(first.astype(jnp.bfloat16), "tensor", axis=0, tiled=True),
        rows,
        preferred_element_type=jnp.float32,
    )
    unused, pull_first = jax.vjp(residual_norm, hidden, mixed, biases[0], gains[0], shifts[0])
    grad_hidden, grad_mixed, bias_one, gain_one, shift_one = pull_first(grad_first)
    piece = lax.all_gather(grad_mixed.astype(jnp.bfloat16), "tensor", axis=0, tiled=True)
    rows = context
    weight_total = jnp.einsum("srd,sre->de", rows, piece, preferred_element_type=jnp.float32)
    update = jnp.einsum("sre,de->srd", piece, out_weight, preferred_element_type=jnp.float32)
    spread = update
    grad_stacked = attend_backward(stacked, allowed, log_total, spread.astype(jnp.bfloat16))
    grad_in_bias = jnp.stack(
        [
            jnp.sum(grad_stacked[0], axis=(0, 1), dtype=jnp.float32),
            jnp.sum(grad_stacked[2], axis=(0, 1), dtype=jnp.float32),
        ]
    )
    part = grad_stacked
    grad_hidden = grad_hidden + lax.psum_scatter(
        jnp.einsum("csre,cde->srd", part, in_weight, preferred_element_type=jnp.float32).astype(
            jnp.bfloat16
        ),
        "tensor",
        scatter_dimension=0,
        tiled=True,
    ).astype(jnp.float32)
    rows = grad_stacked
    grad_in_weight = jnp.einsum(
        "srd,csre->cde",
        lax.all_gather(hidden.astype(jnp.bfloat16), "tensor", axis=0, tiled=True),
        rows,
        preferred_element_type=jnp.float32,
    )
    matrices = (
        grad_in_weight,
        grad_in_bias,
        weight_total,
        grad_wide_weight,
        grad_wide_bias,
        grad_narrow,
    )
    vectors = (
        jnp.stack([bias_one, bias_two]),
        jnp.stack([gain_one, gain_two]),
        jnp.stack([shift_one, shift_two]),
    )
    return (grad_hidden, matrices, vectors)


def local(
    hidden_in,
    cotangent,
    doc_lengths,
    pad_count,
    input_weight,
    input_bias,
    output_weight,
    up_weight,
    up_bias,
    down_weight,
    branch_bias,
    norm_gain,
    norm_shift,
):
    shard_len = hidden_in.shape[0]
    seq_len = shard_len * lax.axis_size("tensor")
    segments = segment_table(doc_lengths, pad_count, seq_len)
    allowed = (segments.T[:, :, None] == segments.T[:, None, :])[:, None]
    layers = input_weight.shape[0]
    stacks = (
        input_weight,
        input_bias,
        output_weight,
        up_weight,
        up_bias,
        down_weight,
        branch_bias.astype(jnp.float32),
        norm_gain.astype(jnp.float32),
        norm_shift.astype(jnp.float32),
    )
    hidden = hidden_in.astype(jnp.float32)
    caches = []
    for layer in range(layers):
        hidden, cache = layer_forward(hidden, allowed, tuple((item[layer] for item in stacks)))
        caches.append(cache)
    hidden_out = hidden.astype(jnp.bfloat16)
    upstream = cotangent.astype(jnp.float32)
    matrix_terms = [None] * layers
    vector_terms = [None] * layers
    for layer in reversed(range(layers)):
        upstream, matrices, vectors = layer_backward(
            upstream, allowed, tuple((item[layer] for item in stacks)), caches[layer]
        )
        matrix_terms[layer] = matrices
        vector_terms[layer] = vectors
    matrix_stack = tuple(
        (jnp.stack([terms[index] for terms in matrix_terms]) for index in range(6))
    )
    vector_stack = tuple(
        (jnp.stack([terms[index] for terms in vector_terms]) for index in range(3))
    )
    matrix_stack = lax.psum(
        (
            matrix_stack[0],
            matrix_stack[1],
            matrix_stack[2],
            matrix_stack[3],
            matrix_stack[4],
            matrix_stack[5],
        ),
        "dp",
    )
    vector_stack = lax.psum((vector_stack[0], vector_stack[1], vector_stack[2]), ("dp", "tensor"))
    return (
        hidden_out,
        upstream,
        matrix_stack[0],
        matrix_stack[1],
        matrix_stack[2],
        matrix_stack[3],
        matrix_stack[4],
        matrix_stack[5],
        vector_stack[0],
        vector_stack[1],
        vector_stack[2],
    )


def solution(mesh):
    return jax.shard_map(
        local,
        mesh=mesh,
        in_specs=(
            P("tensor", "dp", None),
            P("tensor", "dp", None),
            P("dp", None),
            P("dp"),
            P(None, None, None, "tensor"),
            P(None, None, "tensor"),
            P(None, "tensor", None),
            P(None, None, "tensor"),
            P(None, "tensor"),
            P(None, "tensor", None),
            P(),
            P(),
            P(),
        ),
        out_specs=(
            P("tensor", "dp", None),
            P("tensor", "dp", None),
            P(None, None, None, "tensor"),
            P(None, None, "tensor"),
            P(None, "tensor", None),
            P(None, None, "tensor"),
            P(None, "tensor"),
            P(None, "tensor", None),
            P(),
            P(),
            P(),
        ),
        check_vma=False,
    )
```

profile of v0, /device:TPU:0, one launch (start us, length us, event | category | flops | bytes accessed | tf_op | source)
XLA Modules:
  0.0 1003.6 jit_solution(6016320509217997333)
XLA Ops:
  12.0 20.6 %all-gather.9.cloned.1.call-done = bf16[512,2,768]{2,0,1:T(8,128)(2,1)} async-done(((bf16[128,2,768]{2,0,1:T(8,128)(2,1)}), bf16[512,2,768]{2,0,1:T(8,128)(2,1)}) %all-gather.9.cloned.1.call-update) | async-done | bytes 1572880 | tf_op jit(solution)/shard_map/all_gather | solution.py:98
  32.5 2.8 convolution_bitcast_fusion.5
  40.9 2.3 fusion.77
  44.6 36.7 %reduce-scatter.9.cloned.1.call-done = f32[128,2,768]{2,0,1:T(8,128)} async-done(((f32[512,2,768]{2,0,1:T(8,128)}), f32[128,2,768]{2,0,1:T(8,128)}) %reduce-scatter.9.cloned.1.call-update) | async-done | bytes 786448 | tf_op jit(solution)/shard_map/reduce_scatter | solution.py:107
  84.0 19.7 %all-gather.11.cloned.1.call-done = bf16[512,2,768]{2,0,1:T(8,128)(2,1)} async-done(((bf16[128,2,768]{2,0,1:T(8,128)(2,1)}), bf16[512,2,768]{2,0,1:T(8,128)(2,1)}) %all-gather.11.cloned.1.call-update) | async-done | bytes 1572880 | tf_op jit(solution)/shard_map/all_gather | solution.py:117
  103.7 5.0 multiply_convert_fusion.3
  109.9 2.5 convolution_convert_fusion.3
  112.5 28.3 %reduce-scatter.11.cloned.1.call-done = bf16[128,2,768]{2,0,1:T(8,128)(2,1)} async-done(((bf16[512,2,768]{2,0,1:T(8,128)(2,1)}), bf16[128,2,768]{2,0,1:T(8,128)(2,1)}) %reduce-scatter.11.cloned.1.call-update) | async-done | bytes 393232 | tf_op jit(solution)/shard_map/reduce_scatter | solution.py:125
  143.9 19.3 %all-gather.13.cloned.1.call-done = bf16[512,2,768]{2,0,1:T(8,128)(2,1)} async-done(((bf16[128,2,768]{2,0,1:T(8,128)(2,1)}), bf16[512,2,768]{2,0,1:T(8,128)(2,1)}) %all-gather.13.cloned.1.call-update) | async-done | bytes 1572880 | tf_op jit(solution)/shard_map/all_gather | solution.py:98
  163.2 2.7 convolution_bitcast_fusion.4
  171.5 2.3 fusion.74
  173.8 38.0 %reduce-scatter.13.cloned.1.call-done = f32[128,2,768]{2,0,1:T(8,128)} async-done(((f32[512,2,768]{2,0,1:T(8,128)}), f32[128,2,768]{2,0,1:T(8,128)}) %reduce-scatter.13.cloned.1.call-update) | async-done | bytes 786448 | tf_op jit(solution)/shard_map/reduce_scatter | solution.py:107
  214.6 19.8 %all-gather.15.cloned.1.call-done = bf16[512,2,768]{2,0,1:T(8,128)(2,1)} async-done(((bf16[128,2,768]{2,0,1:T(8,128)(2,1)}), bf16[512,2,768]{2,0,1:T(8,128)(2,1)}) %all-gather.15.cloned.1.call-update) | async-done | bytes 1572880 | tf_op jit(solution)/shard_map/all_gather | solution.py:117
  234.4 5.0 multiply_convert_fusion.2
  240.7 2.5 convolution_convert_fusion.2
  243.3 28.3 %reduce-scatter.15.cloned.1.call-done = bf16[128,2,768]{2,0,1:T(8,128)(2,1)} async-done(((bf16[512,2,768]{2,0,1:T(8,128)(2,1)}), bf16[128,2,768]{2,0,1:T(8,128)(2,1)}) %reduce-scatter.15.cloned.1.call-update) | async-done | bytes 393232 | tf_op jit(solution)/shard_map/reduce_scatter | solution.py:125
  274.1 2.1 fusion.98
  277.5 19.6 %all-gather.17.cloned.1.call-done = bf16[512,2,768]{2,0,1:T(8,128)(2,1)} async-done(((bf16[128,2,768]{2,0,1:T(8,128)(2,1)}), bf16[512,2,768]{2,0,1:T(8,128)(2,1)}) %all-gather.17.cloned.1.call-update) | async-done | bytes 1572880 | tf_op jit(solution)/shard_map/all_gather | solution.py:144
  297.1 5.8 convert_reduce_fusion
  304.0 2.6 convolution_convert_fusion.1
  306.7 28.3 %reduce-scatter.17.cloned.1.call-done = bf16[128,2,768]{2,0,1:T(8,128)(2,1)} async-done(((bf16[512,2,768]{2,0,1:T(8,128)(2,1)}), bf16[128,2,768]{2,0,1:T(8,128)(2,1)}) %reduce-scatter.17.cloned.1.call-update) | async-done | bytes 393232 | tf_op jit(solution)/shard_map/reduce_scatter | solution.py:155
  341.1 19.0 %all-gather.19.cloned.1.call-done = bf16[512,2,768]{2,0,1:T(8,128)(2,1)} async-done(((bf16[128,2,768]{2,0,1:T(8,128)(2,1)}), bf16[512,2,768]{2,0,1:T(8,128)(2,1)}) %all-gather.19.cloned.1.call-update) | async-done | bytes 1572880 | tf_op jit(solution)/shard_map/all_gather | solution.py:172
  360.1 2.1 convolution_convert_fusion.5
  362.2 4.8 fusion.28
  367.0 4.3 multiply_reduce_fusion.1
  376.1 2.6 bitcast_convert_fusion.1
  379.0 28.1 %reduce-scatter.19.cloned.1.call-done = bf16[128,2,768]{2,0,1:T(8,128)(2,1)} async-done(((bf16[512,2,768]{2,0,1:T(8,128)(2,1)}), bf16[128,2,768]{2,0,1:T(8,128)(2,1)}) %reduce-scatter.19.cloned.1.call-update) | async-done | bytes 393232 | tf_op jit(solution)/shard_map/reduce_scatter | solution.py:185
  407.1 2.1 multiply_reduce_fusion.3
  411.6 19.8 %all-gather.21.cloned.1.call-done = bf16[512,2,768]{2,0,1:T(8,128)(2,1)} async-done(((bf16[128,2,768]{2,0,1:T(8,128)(2,1)}), bf16[512,2,768]{2,0,1:T(8,128)(2,1)}) %all-gather.21.cloned.1.call-update) | async-done | bytes 1572880 | tf_op jit(solution)/shard_map/all_gather | solution.py:144
  431.3 5.8 convert_reduce_fusion.1
  438.3 2.6 convolution_convert_fusion
  441.0 28.3 %reduce-scatter.21.cloned.1.call-done = bf16[128,2,768]{2,0,1:T(8,128)(2,1)} async-done(((bf16[512,2,768]{2,0,1:T(8,128)(2,1)}), bf16[128,2,768]{2,0,1:T(8,128)(2,1)}) %reduce-scatter.21.cloned.1.call-update) | async-done | bytes 393232 | tf_op jit(solution)/shard_map/reduce_scatter | solution.py:155
  473.2 4.8 convolution_bitcast_fusion
  478.0 14.9 %all-gather.23.cloned.1.call-done = bf16[512,2,768]{2,0,1:T(8,128)(2,1)} async-done(((bf16[128,2,768]{2,0,1:T(8,128)(2,1)}), bf16[512,2,768]{2,0,1:T(8,128)(2,1)}) %all-gather.23.cloned.1.call-update) | async-done | bytes 1572880 | tf_op jit(solution)/shard_map/all_gather | solution.py:172
  493.0 2.1 convolution_convert_fusion.4
  495.1 4.0 fusion.31
  499.1 4.4 multiply_reduce_fusion
  508.0 2.7 bitcast_convert_fusion
  511.2 3.5 convolution_bitcast_fusion.2
  519.7 2.7 pad_maximum_fusion.1
  524.7 2.5 pad_maximum_fusion
  530.5 2.1 pad_maximum_fusion.2
  535.5 43.2 %all-reduce = (f32[2,2,768]{2,1,0:T(2,128)}, f32[2,2,768]{2,1,0:T(2,128)}, f32[2,2,768]{2,1,0:T(2,128)}) all-reduce(f32[2,2,768]{2,1,0:T(2,128)S(1)} %pad_maximum_fusion.10, f32[2,2,768]{2,1,0:T(2,128)S(1)} %pad_maximum_fusion.11, f32[2,2,768]{2,1,0:T(2,128)S(1)} %pad_maximum_fusion.12), channel_id=1, replica_groups=mesh['dp'=8,'tensor'=4] {'dp','tensor'}, use_global_device_ids=true, to_apply=%region_48.49 | all-reduce | flops 9216 | bytes 73728 | tf_op jit(solution)/shard_map/psum | solution.py:279
  579.0 39.0 %all-reduce.1 = (f32[2,2,192]{2,1,0:T(2,128)}, f32[2,768]{1,0:T(2,128)}) all-reduce(f32[2,2,192]{2,1,0:T(2,128)S(1)} %pad_maximum_fusion.14, f32[2,768]{1,0:T(2,128)S(1)} %pad_maximum_fusion.13), channel_id=1, replica_groups=mesh['dp'=8,'tensor'=4] {'dp'}, use_global_device_ids=true, to_apply=%region_37.38 | all-reduce | flops 2304 | bytes 18432 | tf_op jit(solution)/shard_map/psum | solution.py:268
  620.7 365.1 %all-reduce.5.cloned.1.call-done = (f32[2,3,768,192]{2,3,1,0:T(8,128)}, f32[2,192,768]{2,1,0:T(8,128)}, f32[2,768,768]{2,1,0:T(8,128)}, f32[2,768,768]{2,1,0:T(8,128)}) async-done(((f32[2,3,768,192]{2,3,1,0:T(8,128)}, f32[2,192,768]{2,1,0:T(8,128)}, f32[2,768,768]{2,1,0:T(8,128)}, f32[2,768,768]{2,1,0:T(8,128)}), (f32[2,3,768,192]{2,3,1,0:T(8,128)}, f32[2,192,768]{2,1,0:T(8,128)}, f32[2,768,768]{2,1,0:T(8,128)}, ...) | async-done | bytes 14155792 | tf_op jit(solution)/shard_map/psum | solution.py:268
  985.8 4.3 copy.105
  991.1 2.4 copy.107
  994.7 2.2 copy.108
  (361 shorter events, 74.5 us)
Async XLA Ops:
  7.2 25.4 %all-gather.9.cloned.1.call-start = ((), (), s32[]{:S(2)}) async-start(), calls=%async_computation.8 | async-start | bytes 1966080 | tf_op jit(solution)/shard_map/all_gather | solution.py:98
  9.0 72.3 %reduce-scatter.9.cloned.1.call-start = ((), (), s32[]{:S(2)}) async-start(), calls=%async_computation.9 | async-start | bytes 3932160 | tf_op jit(solution)/shard_map/reduce_scatter | solution.py:107
  43.2 38.1 %copy-start.21 = (bf16[128,2,768]{2,1,0:T(2,128)(2,1)S(1)}, bf16[128,2,768]{2,1,0:T(2,128)(2,1)}, u32[]{:S(2)}) copy-start(bf16[128,2,768]{2,1,0:T(2,128)(2,1)} %param.13) | copy-start | bytes 1179652
  43.2 40.7 %copy-start.69 = (bf16[2,768]{1,0:T(2,128)(2,1)S(1)}, bf16[2,768]{1,0:T(2,128)(2,1)}, u32[]{:S(2)}) copy-start(bf16[2,768]{1,0:T(2,128)(2,1)} %param.21) | copy-start | bytes 9220
  43.2 60.5 %all-gather.11.cloned.1.call-start = ((), (), s32[]{:S(2)}) async-start(), calls=%async_computation.10 | async-start | bytes 1966080 | tf_op jit(solution)/shard_map/all_gather | solution.py:117
  44.6 96.2 %copy-start.44 = (f32[768]{0:T(1024)}, f32[768]{0:T(1024)S(1)}, u32[]{:S(2)}) copy-start(f32[768]{0:T(1024)S(1)} %get-tuple-element.114) | copy-start | bytes 9220
  44.6 167.3 %copy-start.46 = (f32[768]{0:T(1024)}, f32[768]{0:T(1024)S(1)}, u32[]{:S(2)}) copy-start(f32[768]{0:T(1024)S(1)} %get-tuple-element.115) | copy-start | bytes 9220
  82.6 58.2 %copy-start.53 = (f32[128,2]{0,1:T(2,128)}, f32[128,2]{0,1:T(2,128)S(1)}, u32[]{:S(2)}) copy-start(f32[128,2]{0,1:T(2,128)S(1)} %broadcast_multiply_fusion.3) | copy-start | bytes 3076
  82.8 25.9 %copy-start.72 = (f32[128,2]{0,1:T(2,128)}, f32[128,2]{0,1:T(2,128)S(1)}, u32[]{:S(2)}) copy-start(f32[128,2]{0,1:T(2,128)S(1)} %multiply_reduce_fusion.11) | copy-start | bytes 3076
  82.9 57.9 %copy-start.57 = (f32[128,2]{0,1:T(2,128)}, f32[128,2]{0,1:T(2,128)S(1)}, u32[]{:S(2)}) copy-start(f32[128,2]{0,1:T(2,128)S(1)} %fusion.84) | copy-start | bytes 3076
  83.9 56.9 %reduce-scatter.11.cloned.1.call-start = ((), (), s32[]{:S(2)}) async-start(), calls=%async_computation.11 | async-start | bytes 1966080 | tf_op jit(solution)/shard_map/reduce_scatter | solution.py:125
  83.9 24.8 %copy-start.80 = (f32[768]{0:T(1024)}, f32[768]{0:T(1024)S(1)}, u32[]{:S(2)}) copy-start(f32[768]{0:T(1024)S(1)} %get-tuple-element.61) | copy-start | bytes 9220
  84.0 150.4 %copy-start.81 = (f32[768]{0:T(1024)}, f32[768]{0:T(1024)S(1)}, u32[]{:S(2)}) copy-start(f32[768]{0:T(1024)S(1)} %get-tuple-element.60) | copy-start | bytes 9220
  112.4 50.8 %all-gather.13.cloned.1.call-start = ((), (), s32[]{:S(2)}) async-start(), calls=%async_computation.12 | async-start | bytes 1966080 | tf_op jit(solution)/shard_map/all_gather | solution.py:98
  142.2 69.7 %copy-start.51 = (f32[128,2]{0,1:T(2,128)}, f32[128,2]{0,1:T(2,128)S(1)}, u32[]{:S(2)}) copy-start(f32[128,2]{0,1:T(2,128)S(1)} %broadcast_multiply_fusion.2) | copy-start | bytes 3076
  142.4 23.6 %copy-start.74 = (f32[128,2]{0,1:T(2,128)}, f32[128,2]{0,1:T(2,128)S(1)}, u32[]{:S(2)}) copy-start(f32[128,2]{0,1:T(2,128)S(1)} %multiply_reduce_fusion.10) | copy-start | bytes 3076
  142.4 69.5 %copy-start.55 = (f32[128,2]{0,1:T(2,128)}, f32[128,2]{0,1:T(2,128)S(1)}, u32[]{:S(2)}) copy-start(f32[128,2]{0,1:T(2,128)S(1)} %fusion.85) | copy-start | bytes 3076
  143.4 68.5 %reduce-scatter.13.cloned.1.call-start = ((), (), s32[]{:S(2)}) async-start(), calls=%async_computation.13 | async-start | bytes 3932160 | tf_op jit(solution)/shard_map/reduce_scatter | solution.py:107
  173.8 60.6 %all-gather.15.cloned.1.call-start = ((), (), s32[]{:S(2)}) async-start(), calls=%async_computation.14 | async-start | bytes 1966080 | tf_op jit(solution)/shard_map/all_gather | solution.py:117
  213.6 25.9 %copy-start.76 = (f32[128,2]{0,1:T(2,128)}, f32[128,2]{0,1:T(2,128)S(1)}, u32[]{:S(2)}) copy-start(f32[128,2]{0,1:T(2,128)S(1)} %multiply_reduce_fusion.9) | copy-start | bytes 3076
  214.6 57.0 %reduce-scatter.15.cloned.1.call-start = ((), (), s32[]{:S(2)}) async-start(), calls=%async_computation.15 | async-start | bytes 1966080 | tf_op jit(solution)/shard_map/reduce_scatter | solution.py:125
  243.2 30.0 %copy-start.22 = (bf16[128,2,768]{2,1,0:T(2,128)(2,1)S(1)}, bf16[128,2,768]{2,1,0:T(2,128)(2,1)}, u32[]{:S(2)}) copy-start(bf16[128,2,768]{2,1,0:T(2,128)(2,1)} %param.14) | copy-start | bytes 1179652
  243.2 53.8 %all-gather.17.cloned.1.call-start = ((), (), s32[]{:S(2)}) async-start(), calls=%async_computation.16 | async-start | bytes 1966080 | tf_op jit(solution)/shard_map/all_gather | solution.py:144
  276.2 58.8 %copy-start.2 = (f32[128,2,768]{2,0,1:T(8,128)}, f32[128,2,768]{2,0,1:T(8,128)S(1)}, u32[]{:S(2)}) copy-start(f32[128,2,768]{2,0,1:T(8,128)S(1)} %get-tuple-element.78) | copy-start | bytes 2359300
  277.2 57.7 %reduce-scatter.17.cloned.1.call-start = ((), (), s32[]{:S(2)}) async-start(), calls=%async_computation.17 | async-start | bytes 1966080 | tf_op jit(solution)/shard_map/reduce_scatter | solution.py:155
  297.0 7.0 copy-start.86
  306.6 53.5 %all-gather.19.cloned.1.call-start = ((), (), s32[]{:S(2)}) async-start(), calls=%async_computation.18 | async-start | bytes 1966080 | tf_op jit(solution)/shard_map/all_gather | solution.py:172
  340.3 66.8 %reduce-scatter.19.cloned.1.call-start = ((), (), s32[]{:S(2)}) async-start(), calls=%async_computation.19 | async-start | bytes 1966080 | tf_op jit(solution)/shard_map/reduce_scatter | solution.py:185
  362.2 9.1 slice-start.2
  376.1 31.0 %copy-start.47 = (f32[768]{0:T(1024)S(1)}, f32[768]{0:T(1024)}, u32[]{:S(2)}) copy-start(f32[768]{0:T(1024)} %copy-done.46) | copy-start | bytes 9220
  376.1 31.0 %copy-start.52 = (f32[128,2]{0,1:T(2,128)S(1)}, f32[128,2]{0,1:T(2,128)}, u32[]{:S(2)}) copy-start(f32[128,2]{0,1:T(2,128)} %copy-done.51) | copy-start | bytes 3076
  376.1 31.0 %copy-start.56 = (f32[128,2]{0,1:T(2,128)S(1)}, f32[128,2]{0,1:T(2,128)}, u32[]{:S(2)}) copy-start(f32[128,2]{0,1:T(2,128)} %copy-done.55) | copy-start | bytes 3076
  376.1 31.0 %copy-start.60 = (f32[128,2]{0,1:T(2,128)S(1)}, f32[128,2]{0,1:T(2,128)}, u32[]{:S(2)}) copy-start(f32[128,2]{0,1:T(2,128)} %copy-done.59) | copy-start | bytes 3076
  378.7 30.4 %copy-start.75 = (f32[128,2]{0,1:T(2,128)S(1)}, f32[128,2]{0,1:T(2,128)}, u32[]{:S(2)}) copy-start(f32[128,2]{0,1:T(2,128)} %copy-done.74) | copy-start | bytes 3076
  378.8 52.6 %all-gather.21.cloned.1.call-start = ((), (), s32[]{:S(2)}) async-start(), calls=%async_computation.20 | async-start | bytes 1966080 | tf_op jit(solution)/shard_map/all_gather | solution.py:144
  411.5 57.7 %reduce-scatter.21.cloned.1.call-start = ((), (), s32[]{:S(2)}) async-start(), calls=%async_computation.21 | async-start | bytes 1966080 | tf_op jit(solution)/shard_map/reduce_scatter | solution.py:155
  431.3 7.0 copy-start.87
  438.3 30.9 %copy-start.45 = (f32[768]{0:T(1024)S(1)}, f32[768]{0:T(1024)}, u32[]{:S(2)}) copy-start(f32[768]{0:T(1024)} %copy-done.44) | copy-start | bytes 9220
  438.3 30.9 %copy-start.54 = (f32[128,2]{0,1:T(2,128)S(1)}, f32[128,2]{0,1:T(2,128)}, u32[]{:S(2)}) copy-start(f32[128,2]{0,1:T(2,128)} %copy-done.53) | copy-start | bytes 3076
  438.3 30.9 %copy-start.58 = (f32[128,2]{0,1:T(2,128)S(1)}, f32[128,2]{0,1:T(2,128)}, u32[]{:S(2)}) copy-start(f32[128,2]{0,1:T(2,128)} %copy-done.57) | copy-start | bytes 3076
  440.9 29.9 %copy-start.73 = (f32[128,2]{0,1:T(2,128)S(1)}, f32[128,2]{0,1:T(2,128)}, u32[]{:S(2)}) copy-start(f32[128,2]{0,1:T(2,128)} %copy-done.72) | copy-start | bytes 3076
  440.9 52.0 %all-gather.23.cloned.1.call-start = ((), (), s32[]{:S(2)}) async-start(), calls=%async_computation.22 | async-start | bytes 1966080 | tf_op jit(solution)/shard_map/all_gather | solution.py:172
  473.1 144.9 %reduce-scatter.23.cloned.1.call-start = ((), (), s32[]{:S(2)}) async-start(), calls=%async_computation.23 | async-start | bytes 1966080 | tf_op jit(solution)/shard_map/reduce_scatter | solution.py:185
  473.2 19.7 %copy-start.36 = (bf16[2,192,768]{2,1,0:T(8,128)(2,1)S(1)}, bf16[2,192,768]{2,1,0:T(8,128)(2,1)}, u32[]{:S(2)}) copy-start(bf16[2,192,768]{2,1,0:T(8,128)(2,1)} %param.19) | copy-start | bytes 1769476
  495.1 8.4 slice-start
  499.1 8.3 copy-start.27
  510.7 475.1 %all-reduce.5.cloned.1.call-start = ((), (), s32[]{:S(2)}) async-start(), calls=%async_computation.24 | async-start | bytes 28311552 | tf_op jit(solution)/shard_map/psum | solution.py:268
  532.7 85.3 %copy-start.71 = (f32[128,2]{0,1:T(2,128)S(1)}, f32[128,2]{0,1:T(2,128)}, u32[]{:S(2)}) copy-start(f32[128,2]{0,1:T(2,128)} %copy-done.70) | copy-start | bytes 3076
  (75 other events, 181.4 us)
Sparse Core Ops, SparseCore 0:
  10.1 22.3 all-gather.8
  43.3 37.9 reduce-scatter.8
  84.0 19.6 all-gather.10
  112.6 28.1 reduce-scatter.10
  143.5 19.6 all-gather.12
  173.9 37.9 reduce-scatter.12
  214.7 19.6 all-gather.14
  243.3 28.1 reduce-scatter.14
  277.4 19.6 all-gather.16
  306.8 28.1 reduce-scatter.16
  340.4 19.6 all-gather.18
  378.9 28.1 reduce-scatter.18
  411.6 19.6 all-gather.20
  441.0 28.1 reduce-scatter.20
  473.3 19.6 all-gather.22
  510.8 28.1 reduce-scatter.22
  544.1 441.5 all-reduce.4
where the time goes:
time: 1010 us; the launch traced here: 1000 us
  waiting for transfers between devices  734 us (73%)
  matrix products  91.8 us (9%)
  blocking collectives  82.3 us (8%)
  other arithmetic  46.3 us (5%)
  local copies, waits for them, and re-layouts  31.8 us (3%)
  between operations  15.5 us (2%)
    psum x1, waiting for transfers between devices, local(): lax.psum((matrix_stack[0], matrix_stack[1], matrix_stack[2], matrix_stack...  365 us
    reduce_scatter x2, waiting for transfers between devices, layer_forward(): lax.psum_scatter(jnp.einsum('srd,de->sre', part, out_weight, preferred_el...  74.8 us
    reduce_scatter x2, waiting for transfers between devices, layer_backward(): lax.psum_scatter(jnp.einsum('srf,df->srd', part, wide_weight, preferred_e...  56.6 us
    reduce_scatter x2, waiting for transfers between devices, layer_forward(): lax.psum_scatter(jnp.einsum('srf,fd->srd', part, narrow_weight, preferred...  56.5 us
    psum x1, blocking collectives, local(): lax.psum((vector_stack[0], vector_stack[1], vector_stack[2]), ('dp', 'ten...  43.2 us
    all_gather x2, waiting for transfers between devices, layer_forward(): lax.all_gather(hidden.astype(jnp.bfloat16), 'tensor', axis=0, tiled=True)  39.9 us
    all_gather x2, waiting for transfers between devices, layer_forward(): lax.all_gather(first.astype(jnp.bfloat16), 'tensor', axis=0, tiled=True)  39.5 us
    all_gather x2, waiting for transfers between devices, layer_backward(): lax.all_gather(grad_fed.astype(jnp.bfloat16), 'tensor', axis=0, tiled=True)  39.4 us
  transfers between devices with their start and end apart: 17, of which 16 were waited for; matrix products, arithmetic and copies ran while one was open for 3% of the time, Pallas kernels for 0%

commit v1 on v0

v1 whole, which is shorter than its diff:
```python
import functools

import jax
import jax.numpy as jnp
from jax import lax
from jax.experimental import pallas as pl
from jax.experimental.pallas import tpu as pltpu
from jax.sharding import PartitionSpec as P

HEAD_DIM = 64
EPSILON = 1e-05
MASKED = -1e30
MESH = pl.DeviceIdType.MESH
BF, F32 = jnp.bfloat16, jnp.float32
NN = (((1,), (0,)), ((), ()))
NT = (((1,), (1,)), ((), ()))
TN = (((0,), (0,)), ((), ()))
UNIT = 384


def dot(a, b, dims):
    return lax.dot_general(a, b, dims, preferred_element_type=F32)


def aligned(value, by=16):
    return pl.multiple_of(value, by)


def segment_table(lengths, padding, seq_len):
    ends = jnp.cumsum(lengths, axis=1)
    position = jnp.arange(seq_len, dtype=jnp.int32)
    index = jnp.sum((position[:, None, None] >= ends[None, :, :]).astype(jnp.int32), axis=2)
    padded = position[:, None] >= (seq_len - padding)[None, :]
    return jnp.where(padded, lengths.shape[1], index)


class Net:
    def __init__(self, n_dp):
        dp, t = lax.axis_index("dp"), lax.axis_index("tensor")
        self.dp, self.t = dp, t
        y, c = t // 2, t % 2
        self.t_core = t + 1 - 2 * c
        self.t_y = t + 2 - 4 * y
        self.t_far = 3 - t
        self.core, self.y = (dp, self.t_core), (dp, self.t_y)
        self.x = dp % 2
        z = (dp // 2) % 4
        self.half = z // 2
        self.inner = (z == 1) | (z == 2)
        self.edge = (z == 0) | (z == 3)
        self.x_dev = (dp + 1 - 2 * self.x, t)
        self.hop_dev = (dp + 2 * (1 - 2 * (z % 2)), t)
        self.mid_dev = (dp + 2 * (3 - 2 * z), t)
        self.z2_dev = (dp + 2 * (2 - 4 * (z // 2)), t)
        self.outer_devs = []
        step = 8
        while step < n_dp:
            self.outer_devs.append((dp + step * (1 - 2 * ((dp // step) % 2)), t))
            step *= 2
        self.vector_devs = [self.x_dev, self.hop_dev, self.z2_dev] + self.outer_devs
        self.partners = [self.core, self.y, self.mid_dev] + self.vector_devs


def remote(src, dst, send, recv, device):
    return pltpu.make_async_remote_copy(
        src_ref=src, dst_ref=dst, send_sem=send, recv_sem=recv, device_id=device, device_id_type=MESH
    )


def kernel(n_dp, layers, *refs):
    (x_in, cot, segc, segr, wt_h, bcol, wo_h, wu_h, wd_h, bup, vec,
     hidden_out, grad_hidden, grads, vectors,
     WT, WO, WU, WD, XG, HG, G, DG, DF, DM, DU, QKVT, PT, CT, DPT, DST, DCT, PART, RB, XRES, HRES, XH, RSTD, GR,
     RX0, RX1, RX2, RZ0, RZ1, RZ2, RXO, RZO, SX0, SX1, SX2, SZ0, SZ1, SZ2, VB, RV,
     wsem, ag_s, ag_r, rs_s, rs_r, arx_s, arx_r, arz_s, arz_r, v_s, v_r, osem) = refs
    DY, DH = XRES, HRES
    net = Net(n_dp)
    rows, block, width = x_in.shape
    seq = PART.shape[1]
    n_qkv = WT.shape[1]
    n_head = n_qkv // 3
    heads = n_head // HEAD_DIM
    ff = WU.shape[2]

    weight_copies = [
        pltpu.make_async_copy(a, b, wsem.at[i])
        for i, (a, b) in enumerate(((wt_h, WT), (wo_h, WO), (wu_h, WU), (wd_h, WD)))
    ]
    for copy in weight_copies:
        copy.start()

    barrier = pltpu.get_barrier_semaphore()
    for device in net.partners:
        pl.semaphore_signal(barrier, inc=1, device_id=device, device_id_type=MESH)
    pl.semaphore_wait(barrier, len(net.partners))

    def rows_at(r, t):
        return pl.ds(aligned(r * seq + t * block), block)

    def mine(r):
        return rows_at(r, net.t)

    ALONG, ACROSS, ONWARD = 0, 1, 2

    def gather_copy(buf, r, k):
        block = buf.at[rows_at(r, net.t_y if k == ONWARD else net.t)]
        return remote(block, block, ag_s.at[r, k], ag_r.at[r, k], net.y if k == ALONG else net.core)

    def gather_start(buf, r):
        gather_copy(buf, r, ALONG).start()
        gather_copy(buf, r, ACROSS).start()

    def gather_pass(buf, r):
        gather_copy(buf, r, ALONG).wait_recv()
        gather_copy(buf, r, ONWARD).start()

    def gather_end(buf, r):
        gather_copy(buf, r, ACROSS).wait_recv()
        gather_copy(buf, r, ONWARD).wait_recv()
        for k in (ALONG, ACROSS, ONWARD):
            gather_copy(buf, r, k).wait_send()

    FAR, NEAR, SUMMED = 0, 1, 2

    def sum_copy(r, k):
        block_of = (net.t_far, net.t_core, net.t_y)[k]
        src = PART.at[r, pl.ds(aligned(block_of * block), block)]
        return remote(src, RB.at[r, k], rs_s.at[r, k], rs_r.at[r, k], net.y if k == SUMMED else net.core)

    def sum_start(r):
        sum_copy(r, FAR).start()
        sum_copy(r, NEAR).start()

    def sum_pass(r):
        sum_copy(r, FAR).wait_recv()
        at = pl.ds(aligned(net.t_y * block), block)
        PART[r, at] = (PART[r, at].astype(F32) + RB[r, FAR].astype(F32)).astype(BF)
        sum_copy(r, SUMMED).start()

    def sum_end(r):
        sum_copy(r, NEAR).wait_recv()
        sum_copy(r, SUMMED).wait_recv()
        for k in (FAR, NEAR, SUMMED):
            sum_copy(r, k).wait_send()
        own = PART[r, pl.ds(aligned(net.t * block), block)]
        return own.astype(F32) + RB[r, NEAR].astype(F32) + RB[r, SUMMED].astype(F32)

    def attention_forward(l, r):
        xg = XG[l, r * seq : (r + 1) * seq]
        for c in range(3):
            at = slice(c * n_head, (c + 1) * n_head)
            QKVT[l, r, at] = (dot(WT[l, at], xg, NT) + bcol[l, at]).astype(BF)

        def head(h, carry):
            o = h * HEAD_DIM
            kt = QKVT[l, r, pl.ds(aligned(n_head + o), HEAD_DIM)] * jnp.asarray(HEAD_DIM**-0.5, BF)
            vt = QKVT[l, r, pl.ds(aligned(2 * n_head + o), HEAD_DIM)]
            qt = QKVT[l, r, pl.ds(aligned(o), HEAD_DIM)]
            scores = jnp.where(segc[r] == segr[r], dot(kt, qt, TN), MASKED)
            powers = jnp.exp(scores - jnp.max(scores, axis=0, keepdims=True))
            probs = (powers * (1.0 / jnp.sum(powers, axis=0, keepdims=True))).astype(BF)
            PT[l, r, h] = probs
            CT[l, r, pl.ds(aligned(o), HEAD_DIM)] = dot(vt, probs, NN).astype(BF)
            return carry

        lax.fori_loop(0, heads, head, 0)
        for q in range(2):
            at = slice(q * seq // 2, (q + 1) * seq // 2)
            PART[r, at] = dot(CT[l, r, :, at], WO[l], TN).astype(BF)

    def norm(l, k, r, value):
        centered = value - jnp.mean(value, axis=-1, keepdims=True)
        rstd = lax.rsqrt(jnp.mean(centered * centered, axis=-1, keepdims=True) + EPSILON)
        normal = centered * rstd
        XH[l, k, r] = normal.astype(BF)
        RSTD[l, k, r] = rstd
        return normal * vec[l, 2 + k : 3 + k] + vec[l, 4 + k : 5 + k]

    def first_norm(l, r):
        out = norm(l, 0, r, XRES[r] + sum_end(r) + vec[l, 0:1])
        HRES[r] = out
        HG[l, mine(r)] = out.astype(BF)
        gather_start(HG.at[l], r)

    def ff_forward(l, r):
        hg = HG[l, r * seq : (r + 1) * seq]
        wide = dot(hg, WU[l], NN) + bup[l]
        cdf = 0.5 * (1.0 + lax.erf(wide * 0.7071067811865476))
        active = (wide * cdf).astype(BF)
        G[l, r * seq : (r + 1) * seq] = active
        DG[l, r * seq : (r + 1) * seq] = (cdf + wide * 0.3989422804014327 * jnp.exp(-0.5 * wide * wide)).astype(BF)
        PART[r] = dot(G[l, r * seq : (r + 1) * seq], WD[l], NN).astype(BF)

    def second_norm(l, r):
        out = norm(l, 1, r, HRES[r] + sum_end(r) + vec[l, 1:2])
        XRES[r] = out

        @pl.when(l < layers - 1)
        def _():
            XG[l + 1, mine(r)] = out.astype(BF)
            gather_start(XG.at[l + 1], r)

        @pl.when(l == layers - 1)
        def _():
            hidden_out[r] = out.astype(BF)

    def norm_backward(l, k, r, upstream):
        normal, rstd = XH[l, k, r].astype(F32), RSTD[l, k, r]
        VB[0, l, 2 + k : 3 + k] += jnp.sum(upstream * normal, axis=0, keepdims=True)
        VB[0, l, 4 + k : 5 + k] += jnp.sum(upstream, axis=0, keepdims=True)
        scaled = upstream * vec[l, 2 + k : 3 + k]
        grad = rstd * (
            scaled
            - jnp.mean(scaled, axis=-1, keepdims=True)
            - normal * jnp.mean(scaled * normal, axis=-1, keepdims=True)
        )
        VB[0, l, k : k + 1] += jnp.sum(grad, axis=0, keepdims=True)
        return grad

    def second_norm_backward(l, r, upstream):
        grad = norm_backward(l, 1, r, upstream)
        DH[r] = grad
        DF[mine(r)] = grad.astype(BF)
        gather_start(DF, r)

    def ff_backward(l, r):
        at = slice(r * seq, (r + 1) * seq)
        grad = (dot(DF[at], WD[l], NT) * DG[l, at].astype(F32)).astype(BF)
        DU[at] = grad
        VB[1, l, 0:1, :ff] += jnp.sum(grad.astype(F32), axis=0, keepdims=True)
        PART[r] = dot(DU[at], WU[l], NT).astype(BF)

    def first_norm_backward(l, r):
        grad = norm_backward(l, 0, r, DH[r] + sum_end(r))
        DY[r] = grad
        DM[mine(r)] = grad.astype(BF)
        gather_start(DM, r)

    def attention_backward(l, r):
        DCT[...] = dot(WO[l], DM[r * seq : (r + 1) * seq], NT).astype(BF)

        def head(h, carry):
            o = h * HEAD_DIM
            q_at, k_at, v_at = (pl.ds(aligned(c * n_head + o), HEAD_DIM) for c in range(3))
            dct = DCT[q_at]
            probs = PT[l, r, h].astype(F32)
            weighted = probs * dot(QKVT[l, r, v_at], dct, TN)
            inner = jnp.sum(weighted, axis=0, keepdims=True)
            DST[...] = (weighted - probs * inner).astype(BF)
            scale = HEAD_DIM**-0.5
            DPT[r, q_at] = (dot(QKVT[l, r, k_at], DST[...], NN) * scale).astype(BF)
            DPT[r, k_at] = (dot(QKVT[l, r, q_at], DST[...], NT) * scale).astype(BF)
            DPT[r, v_at] = dot(dct, PT[l, r, h], NT).astype(BF)
            return carry

        lax.fori_loop(0, heads, head, 0)
        ones = jnp.ones((8, seq), BF)
        VB[1, l, 1:2, :n_qkv] += dot(ones, DPT[r], NT)[0:1]
        for q in range(2):
            at = slice(q * seq // 2, (q + 1) * seq // 2)
            PART[r, at] = dot(DPT[r, :, at], WT[l], TN).astype(BF)

    per_layer = GR.shape[0] // layers

    def tokens_product(left, right, base):
        def strip(i, carry):
            at = pl.ds(aligned(i * 256, 256), 256)
            GR[pl.ds(aligned(base + i * 256), 256)] = dot(left[:, at], right[...], TN).astype(BF)
            return carry

        lax.fori_loop(0, left.shape[1] // 256, strip, 0)

    def attention_gradients(l, base):
        at = pl.ds(aligned(base), n_qkv)
        GR[at] = sum(dot(DPT[r], XG[l, r * seq : (r + 1) * seq], NN) for r in range(rows)).astype(BF)
        at = pl.ds(aligned(base + n_qkv), n_head)
        GR[at] = sum(dot(CT[l, r], DM[r * seq : (r + 1) * seq], NN) for r in range(rows)).astype(BF)

    units = GR.shape[0] // UNIT
    part = UNIT // 2
    half, quarter = part // 2, part // 4
    stages_x, stages_z = [], []
    always = None

    def stage(who_send, who_recv, device, offset, length, landing=None, add=None, staging=None):
        return (who_send, who_recv, device, offset, length, landing, add, staging)

    inner, edge = net.inner, net.edge
    keep, give = net.x * half, (1 - net.x) * half
    keep2, give2 = keep + net.half * quarter, keep + (1 - net.half) * quarter
    stages_x.append(stage(always, always, net.x_dev, give, half, RX0, keep, SX0))
    stages_x.append(stage(edge, inner, net.hop_dev, keep, half, RX1, keep, SX1))
    stages_x.append(stage(inner, inner, net.mid_dev, give2, quarter, RX2, keep2, SX2))
    for i, device in enumerate(net.outer_devs):
        stages_x.append(stage(inner, inner, device, keep2, quarter, RXO.at[i], keep2))
    stages_x.append(stage(inner, inner, net.mid_dev, keep2, quarter))
    stages_x.append(stage(inner, edge, net.hop_dev, keep, half))
    stages_x.append(stage(always, always, net.x_dev, keep, half))
    keep, give = part + net.half * half, part + (1 - net.half) * half
    keep2, give2 = keep + net.x * quarter, keep + (1 - net.x) * quarter
    stages_z.append(stage(edge, inner, net.hop_dev, part, part, RZ0, part, SZ0))
    stages_z.append(stage(inner, inner, net.mid_dev, give, half, RZ1, keep, SZ1))
    stages_z.append(stage(inner, inner, net.x_dev, give2, quarter, RZ2, keep2, SZ2))
    for i, device in enumerate(net.outer_devs):
        stages_z.append(stage(inner, inner, device, keep2, quarter, RZO.at[i], keep2))
    stages_z.append(stage(inner, inner, net.x_dev, keep2, quarter))
    stages_z.append(stage(inner, inner, net.mid_dev, keep, half))
    stages_z.append(stage(inner, edge, net.hop_dev, part, part))
    depth = len(stages_x)

    def when(condition, body):
        if condition is None:
            body()
        else:
            pl.when(condition)(body)

    def stage_copy(which, s, u):
        _, _, device, offset, length, landing, _, staging = which[0][s]
        slot = u % depth
        src = GR.at[pl.ds(aligned(u * UNIT + offset), length)]
        dst = src if landing is None else landing.at[u % landing.shape[0]]
        src = src if staging is None else staging
        return remote(src, dst, which[1].at[slot, s], which[2].at[slot, s], device)

    def stage_send(which, s, u):
        who_send, _, _, offset, length, _, _, staging = which[0][s]

        def send():
            if staging is not None:
                staging[...] = GR[pl.ds(aligned(u * UNIT + offset), length)]
            stage_copy(which, s, u).start()

        when(who_send, send)

    def stage_sent(which, s, u):
        when(which[0][s][0], lambda: stage_copy(which, s, u).wait_send())

    def stage_recv(which, s, u):
        _, who_recv, _, _, length, landing, add, _ = which[0][s]

        def take():
            stage_copy(which, s, u).wait_recv()
            if landing is not None:
                at = pl.ds(aligned(u * UNIT + add), length)
                GR[at] = (GR[at].astype(F32) + landing[u % landing.shape[0]].astype(F32)).astype(BF)

        when(who_recv, take)

    both = ((stages_x, arx_s, arx_r), (stages_z, arz_s, arz_r))

    def out_copy(u):
        at = pl.ds(aligned(u * UNIT), UNIT)
        return pltpu.make_async_copy(GR.at[at], grads.at[at], osem.at[u])

    def tick(t):
        for s in range(depth):
            u = t - 1 - s

            @pl.when((u >= 0) & (u < units))
            def _(s=s, u=u):
                for which in both:
                    stage_sent(which, s, u)

        @pl.when(t < units)
        def _():
            for which in both:
                stage_send(which, 0, t)

        for s in range(depth):
            u = t - 1 - s

            @pl.when((u >= 0) & (u < units))
            def _(s=s, u=u):
                for which in both:
                    stage_recv(which, s, u)
                    if s + 1 < depth:
                        stage_send(which, s + 1, u)
                if s + 1 == depth:
                    out_copy(u).start()

    VB[...] = jnp.zeros(VB.shape, F32)
    for r in range(rows):
        XG[0, mine(r)] = x_in[r]
        XRES[r] = x_in[r].astype(F32)
        gather_start(XG.at[0], r)
    for copy in weight_copies:
        copy.wait()

    def half_layer(buf, compute):
        gather_pass(buf, 0)
        gather_end(buf, 0)
        compute(0)
        sum_start(0)
        gather_pass(buf, 1)
        sum_pass(0)
        gather_end(buf, 1)
        compute(1)
        sum_start(1)
        sum_pass(1)

    def forward(l, carry):
        half_layer(XG.at[l], lambda r: attention_forward(l, r))
        for r in range(rows):
            first_norm(l, r)
        half_layer(HG.at[l], lambda r: ff_forward(l, r))
        for r in range(rows):
            second_norm(l, r)
        return carry

    lax.fori_loop(0, layers, forward, 0)

    per_units = per_layer // UNIT
    for r in range(rows):
        second_norm_backward(layers - 1, r, cot[r].astype(F32))

    def backward(i, carry):
        l = layers - 1 - i
        base, first = i * per_layer, i * per_units
        half_layer(DF, lambda r: ff_backward(l, r))
        tokens_product(G.at[l], DF, base)
        tick(first)
        for r in range(rows):
            first_norm_backward(l, r)
        tokens_product(HG.at[l], DU, base + ff)
        tick(first + 1)
        buf = DM
        gather_pass(buf, 0)
        gather_end(buf, 0)
        attention_backward(l, 0)
        sum_start(0)
        tick(first + 2)
        gather_pass(buf, 1)
        sum_pass(0)
        gather_end(buf, 1)
        attention_backward(l, 1)
        sum_start(1)
        sum_pass(1)
        tick(first + 3)
        attention_gradients(l, base + 2 * ff)
        tick(first + 4)
        for r in range(rows):
            DY[r] = DY[r] + sum_end(r)

            @pl.when(l > 0)
            def _(r=r):
                second_norm_backward(l - 1, r, DY[r])

            @pl.when(l == 0)
            def _(r=r):
                grad_hidden[r] = DY[r]

        tick(first + 5)
        return carry

    lax.fori_loop(0, layers, backward, 0)

    def vector_copy(k):
        if k < 2:
            return remote(VB.at[0], RV.at[k, 0], v_s.at[k], v_r.at[k], (net.core, net.y)[k])
        return remote(VB, RV.at[k], v_s.at[k], v_r.at[k], net.vector_devs[k - 2])

    n_vector = 2 + len(net.vector_devs)
    for k in range(max(depth, n_vector + 1)):
        if 0 < k <= n_vector:
            vector_copy(k - 1).wait()
            if k - 1 < 2:
                VB[0] += RV[k - 1, 0]
            else:
                VB[...] += RV[k - 1]
        if k < n_vector:
            vector_copy(k).start()
        tick(units + k)
    vectors[...] = VB[...]

    def finish(u, carry):
        out_copy(u).wait()
        return carry

    lax.fori_loop(0, units, finish, 0)


def local(
    hidden_in,
    cotangent,
    doc_lengths,
    pad_count,
    input_weight,
    input_bias,
    output_weight,
    up_weight,
    up_bias,
    down_weight,
    branch_bias,
    norm_gain,
    norm_shift,
):
    n_dp = lax.axis_size("dp")
    block, rows, width = hidden_in.shape
    seq = block * lax.axis_size("tensor")
    layers, _, _, n_head = input_weight.shape
    n_qkv, heads, ff = 3 * n_head, n_head // HEAD_DIM, up_weight.shape[2]
    tokens = rows * seq
    segments = segment_table(doc_lengths, pad_count, seq).T
    wt = jnp.swapaxes(input_weight, 2, 3).reshape(layers, n_qkv, width)
    bcol = jnp.stack(
        [input_bias[:, 0], jnp.zeros_like(input_bias[:, 0]), input_bias[:, 1]], axis=1
    ).reshape(layers, n_qkv, 1).astype(F32)
    vec = jnp.concatenate([branch_bias, norm_gain, norm_shift], axis=1).astype(F32)
    per_layer = 2 * ff + n_qkv + n_head
    part = UNIT // 2
    outer = 0
    while 8 << outer < n_dp:
        outer += 1
    depth = 6 + outer
    n_vector = 5 + outer
    vmem = pltpu.VMEM
    dma = pltpu.SemaphoreType.DMA
    scratch = [
        vmem((layers, n_qkv, width), BF),
        vmem((layers, n_head, width), BF),
        vmem((layers, width, ff), BF),
        vmem((layers, ff, width), BF),
        vmem((layers, tokens, width), BF),
        vmem((layers, tokens, width), BF),
        vmem((layers, tokens, ff), BF),
        vmem((layers, tokens, ff), BF),
        vmem((tokens, width), BF),
        vmem((tokens, width), BF),
        vmem((tokens, ff), BF),
        vmem((layers, rows, n_qkv, seq), BF),
        vmem((layers, rows, heads, seq, seq), BF),
        vmem((layers, rows, n_head, seq), BF),
        vmem((rows, n_qkv, seq), BF),
        vmem((seq, seq), BF),
        vmem((n_head, seq), BF),
        vmem((rows, seq, width), BF),
        vmem((rows, 3, block, width), BF),
        vmem((rows, block, width), F32),
        vmem((rows, block, width), F32),
        vmem((layers, 2, rows, block, width), BF),
        vmem((layers, 2, rows, block, 1), F32),
        vmem((layers * per_layer, width), BF),
        vmem((4, part // 2, width), BF),
        vmem((depth, part // 2, width), BF),
        vmem((4, part // 4, width), BF),
        vmem((depth, part, width), BF),
        vmem((4, part // 2, width), BF),
        vmem((4, part // 4, width), BF),
        vmem((max(outer, 1), 4 if outer else 1, part // 4, width), BF),
        vmem((max(outer, 1), 4 if outer else 1, part // 4, width), BF),
        vmem((part // 2, width), BF),
        vmem((part // 2, width), BF),
        vmem((part // 4, width), BF),
        vmem((part, width), BF),
        vmem((part // 2, width), BF),
        vmem((part // 4, width), BF),
        vmem((2, layers, 8, width), F32),
        vmem((n_vector, 2, layers, 8, width), F32),
        dma((4,)),
        dma((rows, 3)),
        dma((rows, 3)),
        dma((rows, 3)),
        dma((rows, 3)),
        dma((depth, depth)),
        dma((depth, depth)),
        dma((depth, depth)),
        dma((depth, depth)),
        dma((n_vector,)),
        dma((n_vector,)),
        dma((layers * per_layer // UNIT,)),
    ]
    whole, anywhere = pl.BlockSpec(memory_space=vmem), pl.BlockSpec(memory_space=pl.ANY)
    hidden_out, grad_hidden, grads, vectors = pl.pallas_call(
        functools.partial(kernel, n_dp, layers),
        out_shape=(
            jax.ShapeDtypeStruct((rows, block, width), BF),
            jax.ShapeDtypeStruct((rows, block, width), F32),
            jax.ShapeDtypeStruct((layers * per_layer, width), BF),
            jax.ShapeDtypeStruct((2, layers, 8, width), F32),
        ),
        in_specs=[whole] * 4 + [anywhere, whole, anywhere, anywhere, anywhere, whole, whole],
        out_specs=(whole, whole, anywhere, whole),
        scratch_shapes=scratch,
        compiler_params=pltpu.CompilerParams(
            collective_id=0, has_side_effects=True, vmem_limit_bytes=63 << 20
        ),
    )(
        jnp.swapaxes(hidden_in, 0, 1),
        jnp.swapaxes(cotangent, 0, 1),
        segments[:, :, None],
        segments[:, None, :],
        wt,
        bcol,
        output_weight,
        up_weight,
        down_weight,
        up_bias.astype(F32)[:, None, :],
        vec,
    )
    grads = grads.reshape(layers, per_layer, width)[::-1]
    grad_in = grads[:, 2 * ff : 2 * ff + n_qkv].reshape(layers, 3, n_head, width)
    shared, split = vectors[0], vectors[1]
    in_bias = split[:, 1, :n_qkv].reshape(layers, 3, n_head)
    return (
        jnp.swapaxes(hidden_out, 0, 1),
        jnp.swapaxes(grad_hidden, 0, 1),
        jnp.swapaxes(grad_in, 2, 3).astype(F32),
        jnp.stack([in_bias[:, 0], in_bias[:, 2]], axis=1),
        grads[:, 2 * ff + n_qkv :].astype(F32),
        grads[:, ff : 2 * ff].astype(F32),
        split[:, 0, :ff],
        grads[:, :ff].astype(F32),
        shared[:, 0:2],
        shared[:, 2:4],
        shared[:, 4:6],
    )


def solution(mesh):
    return jax.shard_map(
        local,
        mesh=mesh,
        in_specs=(
            P("tensor", "dp", None),
            P("tensor", "dp", None),
            P("dp", None),
            P("dp"),
            P(None, None, None, "tensor"),
            P(None, None, "tensor"),
            P(None, "tensor", None),
            P(None, None, "tensor"),
            P(None, "tensor"),
            P(None, "tensor", None),
            P(),
            P(),
            P(),
        ),
        out_specs=(
            P("tensor", "dp", None),
            P("tensor", "dp", None),
            P(None, None, None, "tensor"),
            P(None, None, "tensor"),
            P(None, "tensor", None),
            P(None, None, "tensor"),
            P(None, "tensor"),
            P(None, "tensor", None),
            P(),
            P(),
            P(),
        ),
        check_vma=False,
    )
```

time: 1010 us -> 321 us (0.32)
  waiting for transfers between devices: 734 us -> 0 us
  Pallas kernels: 0 us -> 282 us
  matrix products: 91.8 us -> 0 us
  blocking collectives: 82.3 us -> 0 us
  other arithmetic: 46.3 us -> 13.7 us
  between operations: 15.5 us -> 0.69 us
    psum x1 -> x0, waiting for transfers between devices: 365 us -> none  [local(): lax.psum((matrix_stack[0], matrix_stack[1], matrix_stack[2], matrix_stack...]
    pallas_call x0 -> x1, Pallas kernels: none -> 282 us  [local(): pl.pallas_call(functools.partial(kernel, n_dp, layers), out_shape=(jax.Sh...]
    reduce_scatter x8 -> x0, waiting for transfers between devices: 216 us -> none  [the longest x2 74.8 us: layer_forward(): lax.psum_scatter(jnp.einsum('srd,de->sre', part, out_weight, preferred_el...]
    all_gather x8 -> x0, waiting for transfers between devices: 153 us -> none  [the longest x2 39.9 us: layer_forward(): lax.all_gather(hidden.astype(jnp.bfloat16), 'tensor', axis=0, tiled=True)]
    dot_general x36 -> x0, matrix products: 91.8 us -> none  [the longest x2 11.7 us: layer_backward(): jnp.einsum('srd,fd->srf', piece, narrow_weight, preferred_element_type=jn...]
    psum x2 -> x0, blocking collectives: 82.3 us -> none  [the longest x1 43.2 us: local(): lax.psum((vector_stack[0], vector_stack[1], vector_stack[2]), ('dp', 'ten...]
    unnamed x219 -> x7, local copies, waits for them, and re-layouts: 30.9 us -> 5.4 us
    reduce_sum x23 -> x0, other arithmetic: 22.8 us -> none  [the longest x4 6.7 us: normalize(): centered = value - average]
  transfers between devices with their start and end apart: 17 -> 0, of which waited for: 16 -> 0; matrix products, arithmetic and copies ran while one was open for 3% -> 0% of each run, Pallas kernels for 0% -> 0%
where the time goes in v1:
time: 321 us; the launch traced here: 320 us
  Pallas kernels  282 us (88%)
  local copies, waits for them, and re-layouts  24.1 us (8%)
  other arithmetic  13.7 us (4%)
    pallas_call x1, Pallas kernels, local(): pl.pallas_call(functools.partial(kernel, n_dp, layers), out_shape=(jax.Sh...  282 us

profile of v1, /device:TPU:0, one launch (start us, length us, event | category | flops | bytes accessed | tf_op | source)
XLA Modules:
  0.0 320.1 jit_solution(11745497373335188329)
XLA Ops:
  0.6 0.7 broadcast_subtract_fusion
  1.3 0.1 pad.6.clone
  1.4 0.8 reduce_window_sum.11
  2.2 0.1 copy.37
  2.3 0.1 fusion
  2.4 0.1 fusion.5
  2.5 0.1 compare_select_fusion
  2.6 0.6 broadcast_in_dim.21.refs_3_
  3.2 0.8 fusion.4
  3.9 0.1 maximum_convert_fusion.1
  4.0 1.3 reshape.53.refs_9_
  5.3 1.4 maximum_convert_fusion.refs_10_
  6.6 1.0 copy.38.refs_2_
  7.7 1.3 reshape.55.refs_5_
  8.9 2.1 copy_bitcast_fusion
  11.0 281.6 %shard_map.212 = (bf16[2,128,768]{2,1,0:T(8,128)(2,1)}, f32[2,128,768]{2,1,0:T(8,128)}, bf16[4608,768]{1,0:T(8,128)(2,1)}, f32[2,2,8,768]{3,2,1,0:T(8,128)}) custom-call(bf16[2,128,768]{2,1,0:T(8,128)(2,1)} %get-tuple-element.64.refs_0_, bf16[2,128,768]{2,1,0:T(8,128)(2,1)} %get-tuple-element.63.refs_1_, s32[2,512,1]{2,1,0:T(8,128)} %copy.38.refs_2_, ...), custom_call_target="tpu_custom_call" | custom-call | tf_op jit(solution)/shard_map/pallas_call | solution.py:573
  292.6 0.0 copy-start.1
  292.7 2.2 copy.40
  294.8 2.6 copy.41
  297.5 0.0 copy-done.1
  297.5 0.6 fusion.2
  298.1 0.6 copy.46
  298.7 0.1 reshape_squeeze.3
  298.8 0.6 pad_maximum_fusion
  299.4 1.1 slice.80
  300.5 1.1 reverse_convert_fusion.2
  301.6 2.8 slice.76
  304.4 4.1 %fusion.1 = (bf16[2,768,768]{2,1,0:T(8,128)(2,1)}, bf16[2,768,768]{2,1,0:T(8,128)(2,1)S(1)}) fusion(bf16[2,2304,768]{2,1,0:T(8,128)(2,1)} %bitcast.30), kind=kLoop, calls=%fused_computation.17 | loop fusion | bytes 9437184 | tf_op jit(solution)/shard_map/slice | solution.py:612
  308.5 2.8 slice.60
  311.3 0.0 copy-start
  311.3 3.7 %convert_bitcast_fusion = f32[2,3,768,192]{2,3,1,0:T(8,128)} fusion(bf16[2,3,192,768]{3,2,1,0:T(8,128)(2,1)} %bitcast.31), kind=kLoop, calls=%fused_computation | loop fusion | flops 884736 | bytes 5308416 | tf_op jit(solution)/shard_map/convert_element_type | solution.py:607
  315.0 0.0 copy-done
  315.0 2.5 reverse_convert_fusion
  317.6 2.5 reverse_convert_fusion.1
  (4 shorter events, 0.0 us)
Async XLA Ops:
  292.6 4.8 %copy-start.1 = (f32[2,2,8,768]{3,2,1,0:T(8,128)S(1)}, f32[2,2,8,768]{3,2,1,0:T(8,128)}, u32[]{:S(2)}) copy-start(f32[2,2,8,768]{3,2,1,0:T(8,128)} %get-tuple-element.18) | copy-start | bytes 294916
  311.3 3.7 %copy-start = (bf16[2,768,768]{2,1,0:T(8,128)(2,1)S(1)}, bf16[2,768,768]{2,1,0:T(8,128)(2,1)}, u32[]{:S(2)}) copy-start(bf16[2,768,768]{2,1,0:T(8,128)(2,1)} %get-tuple-element.52) | copy-start | bytes 7077892

commit v2 on v1

--- a/solution.py
+++ b/solution.py
@@ -15,7 +15,8 @@
 NN = (((1,), (0,)), ((), ()))
 NT = (((1,), (1,)), ((), ()))
 TN = (((0,), (0,)), ((), ()))
-UNIT = 384
+UNIT = 128
+SPACING, SLOTS = 2, 6
 
 
 def dot(a, b, dims):
@@ -24,14 +25,6 @@
 
 def aligned(value, by=16):
     return pl.multiple_of(value, by)
-
-
-def segment_table(lengths, padding, seq_len):
-    ends = jnp.cumsum(lengths, axis=1)
-    position = jnp.arange(seq_len, dtype=jnp.int32)
-    index = jnp.sum((position[:, None, None] >= ends[None, :, :]).astype(jnp.int32), axis=2)
-    padded = position[:, None] >= (seq_len - padding)[None, :]
-    return jnp.where(padded, lengths.shape[1], index)
 
 
 class Net:
@@ -68,14 +61,15 @@
 
 
 def kernel(n_dp, layers, *refs):
-    (x_in, cot, segc, segr, wt_h, bcol, wo_h, wu_h, wd_h, bup, vec,
-     hidden_out, grad_hidden, grads, vectors,
-     WT, WO, WU, WD, XG, HG, G, DG, DF, DM, DU, QKVT, PT, CT, DPT, DST, DCT, PART, RB, XRES, HRES, XH, RSTD, GR,
-     RX0, RX1, RX2, RZ0, RZ1, RZ2, RXO, RZO, SX0, SX1, SX2, SZ0, SZ1, SZ2, VB, RV,
-     wsem, ag_s, ag_r, rs_s, rs_r, arx_s, arx_r, arz_s, arz_r, v_s, v_r, osem) = refs
+    (x_in, cot, lengths, padding, wt_h, in_bias, wo_h, wu_h, up_bias, wd_h, branch_bias, norm_gain, norm_shift,
+     hidden_out, grad_hidden, grad_in, grad_in_bias, grad_out, grad_up, grad_up_bias, grad_down,
+     grad_branch, grad_gain, grad_shift,
+     WT, WO, WU, WD, XG, HG, G, DG, DF, DU, QKVT, PT, CT, DPT, DST, DCT, PART, RB, XRES, HRES, XH, RSTD, GR,
+     RX0, RX1, RX2, RZ0, RZ1, RZ2, RXO, RZO, SX0, SX1, SZ0, SZ1, VB, RV, segc, segr, bcol, bup, vec,
+     wsem, ag_s, ag_r, rs_s, rs_r, arx_s, arx_r, arz_s, arz_r, v_s, v_r, osem, credit_x, credit_z) = refs
     DY, DH = XRES, HRES
     net = Net(n_dp)
-    rows, block, width = x_in.shape
+    block, rows, width = x_in.shape
     seq = PART.shape[1]
     n_qkv = WT.shape[1]
     n_head = n_qkv // 3
@@ -184,7 +178,7 @@
 
     def ff_forward(l, r):
         hg = HG[l, r * seq : (r + 1) * seq]
-        wide = dot(hg, WU[l], NN) + bup[l]
+        wide = dot(hg, WU[l], NN) + bup[l, 0:1]
         cdf = 0.5 * (1.0 + lax.erf(wide * 0.7071067811865476))
         active = (wide * cdf).astype(BF)
         G[l, r * seq : (r + 1) * seq] = active
@@ -202,7 +196,7 @@
 
         @pl.when(l == layers - 1)
         def _():
-            hidden_out[r] = out.astype(BF)
+            hidden_out[:, r, :] = out.astype(BF)
 
     def norm_backward(l, k, r, upstream):
         normal, rstd = XH[l, k, r].astype(F32), RSTD[l, k, r]
@@ -233,11 +227,11 @@
     def first_norm_backward(l, r):
         grad = norm_backward(l, 0, r, DH[r] + sum_end(r))
         DY[r] = grad
-        DM[mine(r)] = grad.astype(BF)
-        gather_start(DM, r)
+        DG[l, mine(r)] = grad.astype(BF)
+        gather_start(DG.at[l], r)
 
     def attention_backward(l, r):
-        DCT[...] = dot(WO[l], DM[r * seq : (r + 1) * seq], NT).astype(BF)
+        DCT[...] = dot(WO[l], DG[l, r * seq : (r + 1) * seq], NT).astype(BF)
 
         def head(h, carry):
             o = h * HEAD_DIM
@@ -274,11 +268,11 @@
         at = pl.ds(aligned(base), n_qkv)
         GR[at] = sum(dot(DPT[r], XG[l, r * seq : (r + 1) * seq], NN) for r in range(rows)).astype(BF)
         at = pl.ds(aligned(base + n_qkv), n_head)
-        GR[at] = sum(dot(CT[l, r], DM[r * seq : (r + 1) * seq], NN) for r in range(rows)).astype(BF)
+        GR[at] = sum(dot(CT[l, r], DG[l, r * seq : (r + 1) * seq], NN) for r in range(rows)).astype(BF)
 
     units = GR.shape[0] // UNIT
     part = UNIT // 2
-    half, quarter = part // 2, part // 4
+    half = part // 2
     stages_x, stages_z = [], []
     always = None
 
@@ -287,26 +281,23 @@
 
     inner, edge = net.inner, net.edge
     keep, give = net.x * half, (1 - net.x) * half
-    keep2, give2 = keep + net.half * quarter, keep + (1 - net.half) * quarter
     stages_x.append(stage(always, always, net.x_dev, give, half, RX0, keep, SX0))
     stages_x.append(stage(edge, inner, net.hop_dev, keep, half, RX1, keep, SX1))
-    stages_x.append(stage(inner, inner, net.mid_dev, give2, quarter, RX2, keep2, SX2))
+    stages_x.append(stage(inner, inner, net.mid_dev, keep, half, RX2, keep))
     for i, device in enumerate(net.outer_devs):
-        stages_x.append(stage(inner, inner, device, keep2, quarter, RXO.at[i], keep2))
-    stages_x.append(stage(inner, inner, net.mid_dev, keep2, quarter))
+        stages_x.append(stage(inner, inner, device, keep, half, RXO.at[i], keep))
     stages_x.append(stage(inner, edge, net.hop_dev, keep, half))
     stages_x.append(stage(always, always, net.x_dev, keep, half))
     keep, give = part + net.half * half, part + (1 - net.half) * half
-    keep2, give2 = keep + net.x * quarter, keep + (1 - net.x) * quarter
     stages_z.append(stage(edge, inner, net.hop_dev, part, part, RZ0, part, SZ0))
     stages_z.append(stage(inner, inner, net.mid_dev, give, half, RZ1, keep, SZ1))
-    stages_z.append(stage(inner, inner, net.x_dev, give2, quarter, RZ2, keep2, SZ2))
+    stages_z.append(stage(inner, inner, net.x_dev, keep, half, RZ2, keep))
     for i, device in enumerate(net.outer_devs):
-        stages_z.append(stage(inner, inner, device, keep2, quarter, RZO.at[i], keep2))
-    stages_z.append(stage(inner, inner, net.x_dev, keep2, quarter))
+        stages_z.append(stage(inner, inner, device, keep, half, RZO.at[i], keep))
     stages_z.append(stage(inner, inner, net.mid_dev, keep, half))
     stages_z.append(stage(inner, edge, net.hop_dev, part, part))
     depth = len(stages_x)
+    hops = {0: (stages_z, credit_z), 1: (stages_x, credit_x)}
 
     def when(condition, body):
         if condition is None:
@@ -316,18 +307,26 @@
 
     def stage_copy(which, s, u):
         _, _, device, offset, length, landing, _, staging = which[0][s]
-        slot = u % depth
         src = GR.at[pl.ds(aligned(u * UNIT + offset), length)]
-        dst = src if landing is None else landing.at[u % landing.shape[0]]
-        src = src if staging is None else staging
-        return remote(src, dst, which[1].at[slot, s], which[2].at[slot, s], device)
+        dst = src if landing is None else landing.at[u % SLOTS]
+        src = src if staging is None else staging.at[u % SPACING]
+        return remote(src, dst, which[1].at[u, s], which[2].at[u, s], device)
+
+    def credit_of(which, s):
+        return hops[s][1] if s in hops and hops[s][0] is which[0] else None
 
     def stage_send(which, s, u):
         who_send, _, _, offset, length, _, _, staging = which[0][s]
 
         def send():
+            if credit_of(which, s) is not None:
+
+                @pl.when(u >= SLOTS)
+                def _():
+                    pl.semaphore_wait(credit_of(which, s), 1)
+
             if staging is not None:
-                staging[...] = GR[pl.ds(aligned(u * UNIT + offset), length)]
+                staging[u % SPACING] = GR[pl.ds(aligned(u * UNIT + offset), length)]
             stage_copy(which, s, u).start()
 
         when(who_send, send)
@@ -336,38 +335,66 @@
         when(which[0][s][0], lambda: stage_copy(which, s, u).wait_send())
 
     def stage_recv(which, s, u):
-        _, who_recv, _, _, length, landing, add, _ = which[0][s]
+        _, who_recv, device, _, length, landing, add, _ = which[0][s]
 
         def take():
             stage_copy(which, s, u).wait_recv()
             if landing is not None:
                 at = pl.ds(aligned(u * UNIT + add), length)
-                GR[at] = (GR[at].astype(F32) + landing[u % landing.shape[0]].astype(F32)).astype(BF)
+                GR[at] = (GR[at].astype(F32) + landing[u % SLOTS].astype(F32)).astype(BF)
+            if credit_of(which, s) is not None:
+
+                @pl.when(u < units - SLOTS)
+                def _():
+                    pl.semaphore_signal(credit_of(which, s), inc=1, device_id=device, device_id_type=MESH)
 
         when(who_recv, take)
 
     both = ((stages_x, arx_s, arx_r), (stages_z, arz_s, arz_r))
-
-    def out_copy(u):
-        at = pl.ds(aligned(u * UNIT), UNIT)
-        return pltpu.make_async_copy(GR.at[at], grads.at[at], osem.at[u])
-
-    def tick(t):
+    per_units = per_layer // UNIT
+    sections = (
+        (ff // UNIT, grad_down, 0),
+        (2 * ff // UNIT, grad_up, ff),
+        (per_units, grad_in, 2 * ff),
+        (per_units, grad_out, 2 * ff + n_qkv),
+    )
+    at_place = (2, 1, 1, 1, 1, 1, 1, 1, 2, 1, 1, 1, 1, 2, 1)
+    before = [sum(at_place[:e]) * per_units // sum(at_place) for e in range(len(at_place) + 1)]
+    down_done, up_done, all_done = 4, 6, 13
+    lag = before[down_done]
+    assert before[up_done] <= lag + ff // UNIT and before[all_done] <= lag + 2 * ff // UNIT
+
+    def out_copy(i, k):
+        _, out, base = sections[k]
+        out = out.at[layers - 1 - i]
+        src = GR.at[pl.ds(aligned(i * per_layer + base), out.shape[0])]
+        return pltpu.make_async_copy(src, out, osem.at[i, k])
+
+    def unit_done(u):
+        i, own = u // per_units, u % per_units
+        for k, (end, _, _) in enumerate(sections):
+
+            @pl.when(own == end - 1)
+            def _(k=k):
+                out_copy(i, k).start()
+
+    def tick(now, carry=0):
+        t = now - lag
         for s in range(depth):
-            u = t - 1 - s
+            u = t - SPACING * (s + 1)
 
             @pl.when((u >= 0) & (u < units))
             def _(s=s, u=u):
                 for which in both:
                     stage_sent(which, s, u)
 
-        @pl.when(t < units)
+        @pl.when((t >= 0) & (t < units))
         def _():
             for which in both:
                 stage_send(which, 0, t)
 
         for s in range(depth):
-            u = t - 1 - s
+            u = t - SPACING * (s + 1)
 
             @pl.when((u >= 0) & (u < units))
             def _(s=s, u=u):
@@ -376,13 +403,37 @@
                     if s + 1 < depth:
                         stage_send(which, s + 1, u)
                 if s + 1 == depth:
-                    out_copy(u).start()
+                    unit_done(u)
+
+        return carry
+
+    for r in range(rows):
+        XG[0, mine(r)] = x_in[:, r, :]
+        gather_start(XG.at[0], r)
 
     VB[...] = jnp.zeros(VB.shape, F32)
+    diagonal = lax.broadcasted_iota(jnp.int32, (n_head, n_head), 0) == lax.broadcasted_iota(
+        jnp.int32, (n_head, n_head), 1
+    )
+    for l in range(layers):
+        vec[l, 0:2] = branch_bias[l].astype(F32)
+        vec[l, 2:4] = norm_gain[l].astype(F32)
+        vec[l, 4:6] = norm_shift[l].astype(F32)
+        bup[l, 0:1] = up_bias[l : l + 1].astype(F32)
+        for c, at in ((0, 0), (1, 2 * n_head)):
+            spread = jnp.where(diagonal, in_bias[l, c : c + 1].astype(F32), 0.0)
+            bcol[l, at : at + n_head] = jnp.sum(spread, axis=1, keepdims=True)
+        bcol[l, n_head : 2 * n_head] = jnp.zeros((n_head, 1), F32)
     for r in range(rows):
-        XG[0, mine(r)] = x_in[r]
-        XRES[r] = x_in[r].astype(F32)
-        gather_start(XG.at[0], r)
+        for ref, shape, axis in ((segc, (seq, 1), 0), (segr, (1, seq), 1)):
+            position = lax.broadcasted_iota(jnp.int32, shape, axis)
+            index, end = jnp.zeros(shape, jnp.int32), 0
+            for j in range(lengths.shape[1]):
+                end = end + lengths[r, j]
+                index = index + jnp.where(position >= end, 1, 0)
+            ref[r] = jnp.where(position >= seq - padding[r], lengths.shape[1], index)
+    for r in range(rows):
+        XRES[r] = XG[0, mine(r)].astype(F32)
     for copy in weight_copies:
         copy.wait()
 
@@ -409,35 +460,57 @@
 
     lax.fori_loop(0, layers, forward, 0)
 
-    per_units = per_layer // UNIT
     for r in range(rows):
-        second_norm_backward(layers - 1, r, cot[r].astype(F32))
+        second_norm_backward(layers - 1, r, cot[:, r, :].astype(F32))
 
     def backward(i, carry):
         l = layers - 1 - i
-        base, first = i * per_layer, i * per_units
-        half_layer(DF, lambda r: ff_backward(l, r))
+        base = i * per_layer
+
+        def place(e):
+            for k in range(before[e], before[e + 1]):
+                tick(i * per_units + k)
+
+        place(0)
+        gather_pass(DF, 0)
+        place(1)
+        gather_end(DF, 0)
+        ff_backward(l, 0)
+        sum_start(0)
+        place(2)
+        gather_pass(DF, 1)
+        sum_pass(0)
+        place(3)
+        gather_end(DF, 1)
         tokens_product(G.at[l], DF, base)
-        tick(first)
-        for r in range(rows):
-            first_norm_backward(l, r)
+        place(4)
+        ff_backward(l, 1)
+        sum_start(1)
+        place(5)
+        sum_pass(1)
         tokens_product(HG.at[l], DU, base + ff)
-        tick(first + 1)
-        buf = DM
+        place(6)
+        first_norm_backward(l, 0)
+        place(7)
+        first_norm_backward(l, 1)
+        place(8)
+        buf = DG.at[l]
         gather_pass(buf, 0)
+        place(9)
         gather_end(buf, 0)
         attention_backward(l, 0)
         sum_start(0)
-        tick(first + 2)
+        place(10)
         gather_pass(buf, 1)
         sum_pass(0)
+        place(11)
         gather_end(buf, 1)
         attention_backward(l, 1)
         sum_start(1)
+        place(12)
         sum_pass(1)
-        tick(first + 3)
         attention_gradients(l, base + 2 * ff)
-        tick(first + 4)
+        place(13)
         for r in range(rows):
             DY[r] = DY[r] + sum_end(r)
 
@@ -447,9 +520,11 @@
 
             @pl.when(l == 0)
             def _(r=r):
-                grad_hidden[r] = DY[r]
-
-        tick(first + 5)
+                grad_hidden[:, r, :] = DY[r]
+
+            if r == 0:
+                place(14)
+
         return carry
 
     lax.fori_loop(0, layers, backward, 0)
@@ -460,8 +535,9 @@
         return remote(VB, RV.at[k], v_s.at[k], v_r.at[k], net.vector_devs[k - 2])
 
     n_vector = 2 + len(net.vector_devs)
-    for k in range(max(depth, n_vector + 1)):
-        if 0 < k <= n_vector:
+    now, last = layers * per_units, lag + units + SPACING * depth
+    for k in range(n_vector + 1):
+        if k > 0:
             vector_copy(k - 1).wait()
             if k - 1 < 2:
                 VB[0] += RV[k - 1, 0]
@@ -469,14 +545,19 @@
                 VB[...] += RV[k - 1]
         if k < n_vector:
             vector_copy(k).start()
-        tick(units + k)
-    vectors[...] = VB[...]
-
-    def finish(u, carry):
-        out_copy(u).wait()
-        return carry
-
-    lax.fori_loop(0, units, finish, 0)
+        lax.fori_loop(now, now + 2, tick, 0)
+        now += 2
+    lax.fori_loop(now, last, tick, 0)
+    for l in range(layers):
+        grad_branch[l] = VB[0, l, 0:2]
+        grad_gain[l] = VB[0, l, 2:4]
+        grad_shift[l] = VB[0, l, 4:6]
+        grad_up_bias[l : l + 1] = VB[1, l, 0:1, :ff]
+        for c, at in ((0, 0), (1, 2 * n_head)):
+            grad_in_bias[l, c : c + 1] = VB[1, l, 1:2, at : at + n_head]
+    for i in range(layers):
+        for k in range(len(sections)):
+            out_copy(i, k).wait()
 
 
 def local(
@@ -500,18 +581,13 @@
     layers, _, _, n_head = input_weight.shape
     n_qkv, heads, ff = 3 * n_head, n_head // HEAD_DIM, up_weight.shape[2]
     tokens = rows * seq
-    segments = segment_table(doc_lengths, pad_count, seq).T
     wt = jnp.swapaxes(input_weight, 2, 3).reshape(layers, n_qkv, width)
-    bcol = jnp.stack(
-        [input_bias[:, 0], jnp.zeros_like(input_bias[:, 0]), input_bias[:, 1]], axis=1
-    ).reshape(layers, n_qkv, 1).astype(F32)
-    vec = jnp.concatenate([branch_bias, norm_gain, norm_shift], axis=1).astype(F32)
     per_layer = 2 * ff + n_qkv + n_head
     part = UNIT // 2
     outer = 0
     while 8 << outer < n_dp:
         outer += 1
-    depth = 6 + outer
+    depth = 5 + outer
     n_vector = 5 + outer
     vmem = pltpu.VMEM
     dma = pltpu.SemaphoreType.DMA
@@ -524,7 +600,6 @@
         vmem((layers, tokens, width), BF),
         vmem((layers, tokens, ff), BF),
         vmem((layers, tokens, ff), BF),
-        vmem((tokens, width), BF),
         vmem((tokens, width), BF),
         vmem((tokens, ff), BF),
         vmem((layers, rows, n_qkv, seq), BF),
@@ -540,79 +615,104 @@
         vmem((layers, 2, rows, block, width), BF),
         vmem((layers, 2, rows, block, 1), F32),
         vmem((layers * per_layer, width), BF),
-        vmem((4, part // 2, width), BF),
-        vmem((depth, part // 2, width), BF),
-        vmem((4, part // 4, width), BF),
-        vmem((depth, part, width), BF),
-        vmem((4, part // 2, width), BF),
-        vmem((4, part // 4, width), BF),
-        vmem((max(outer, 1), 4 if outer else 1, part // 4, width), BF),
-        vmem((max(outer, 1), 4 if outer else 1, part // 4, width), BF),
-        vmem((part // 2, width), BF),
-        vmem((part // 2, width), BF),
-        vmem((part // 4, width), BF),
-        vmem((part, width), BF),
-        vmem((part // 2, width), BF),
-        vmem((part // 4, width), BF),
+        vmem((SLOTS, part // 2, width), BF),
+        vmem((SLOTS, part // 2, width), BF),
+        vmem((SLOTS, part // 2, width), BF),
+        vmem((SLOTS, part, width), BF),
+        vmem((SLOTS, part // 2, width), BF),
+        vmem((SLOTS, part // 2, width), BF),
+        vmem((max(outer, 1), SLOTS if outer else 1, part // 2, width), BF),
+        vmem((max(outer, 1), SLOTS if outer else 1, part // 2, width), BF),
+        vmem((SPACING, part // 2, width), BF),
+        vmem((SPACING, part // 2, width), BF),
+        vmem((SPACING, part, width), BF),
+        vmem((SPACING, part // 2, width), BF),
         vmem((2, layers, 8, width), F32),
         vmem((n_vector, 2, layers, 8, width), F32),
+        vmem((rows, seq, 1), jnp.int32),
+        vmem((rows, 1, seq), jnp.int32),
+        vmem((layers, n_qkv, 1), F32),
+        vmem((layers, 8, ff), F32),
+        vmem((layers, 8, width), F32),
         dma((4,)),
         dma((rows, 3)),
         dma((rows, 3)),
         dma((rows, 3)),
         dma((rows, 3)),
-        dma((depth, depth)),
-        dma((depth, depth)),
-        dma((depth, depth)),
-        dma((depth, depth)),
+        dma((layers * per_layer // UNIT, depth)),
+        dma((layers * per_layer // UNIT, depth)),
+        dma((layers * per_layer // UNIT, depth)),
+        dma((layers * per_layer // UNIT, depth)),
         dma((n_vector,)),
         dma((n_vector,)),
-        dma((layers * per_layer // UNIT,)),
+        dma((layers, 4)),
+        pltpu.SemaphoreType.REGULAR,
+        pltpu.SemaphoreType.REGULAR,
     ]
     whole, anywhere = pl.BlockSpec(memory_space=vmem), pl.BlockSpec(memory_space=pl.ANY)
-    hidden_out, grad_hidden, grads, vectors = pl.pallas_call(
+    scalars = pl.BlockSpec(memory_space=pltpu.SMEM)
+    (
+        hidden_out,
+        grad_hidden,
+        grad_in,
+        grad_in_bias,
+        grad_out,
+        grad_up,
+        grad_up_bias,
+        grad_down,
+        grad_branch,
+        grad_gain,
+        grad_shift,
+    ) = pl.pallas_call(
         functools.partial(kernel, n_dp, layers),
         out_shape=(
-            jax.ShapeDtypeStruct((rows, block, width), BF),
-            jax.ShapeDtypeStruct((rows, block, width), F32),
-            jax.ShapeDtypeStruct((layers * per_layer, width), BF),
-            jax.ShapeDtypeStruct((2, layers, 8, width), F32),
+            jax.ShapeDtypeStruct(hidden_in.shape, BF),
+            jax.ShapeDtypeStruct(hidden_in.shape, F32),
+            jax.ShapeDtypeStruct((layers, n_qkv, width), BF),
+            jax.ShapeDtypeStruct(input_bias.shape, F32),
+            jax.ShapeDtypeStruct(output_weight.shape, BF),
+            jax.ShapeDtypeStruct(up_weight.shape, BF),
+            jax.ShapeDtypeStruct(up_bias.shape, F32),
+            jax.ShapeDtypeStruct(down_weight.shape, BF),
+            jax.ShapeDtypeStruct(branch_bias.shape, F32),
+            jax.ShapeDtypeStruct(norm_gain.shape, F32),
+            jax.ShapeDtypeStruct(norm_shift.shape, F32),
         ),
-        in_specs=[whole] * 4 + [anywhere, whole, anywhere, anywhere, anywhere, whole, whole],
-        out_specs=(whole, whole, anywhere, whole),
+        in_specs=[whole, whole, scalars, scalars, anywhere, whole, anywhere, anywhere, whole, anywhere]
+        + [whole] * 3,
+        out_specs=(whole, whole, anywhere, whole, anywhere, anywhere, whole, anywhere, whole, whole, whole),
         scratch_shapes=scratch,
         compiler_params=pltpu.CompilerParams(
             collective_id=0, has_side_effects=True, vmem_limit_bytes=63 << 20
         ),
     )(
-        jnp.swapaxes(hidden_in, 0, 1),
-        jnp.swapaxes(cotangent, 0, 1),
-        segments[:, :, None],
-        segments[:, None, :],
+        hidden_in,
+        cotangent,
+        doc_lengths,
+        pad_count,
         wt,
-        bcol,
+        input_bias,
         output_weight,
         up_weight,
+        up_bias,
         down_weight,
-        up_bias.astype(F32)[:, None, :],
-        vec,
+        branch_bias,
+        norm_gain,
+        norm_shift,
     )
-    grads = grads.reshape(layers, per_layer, width)[::-1]
-    grad_in = grads[:, 2 * ff : 2 * ff + n_qkv].reshape(layers, 3, n_head, width)
-    shared, split = vectors[0], vectors[1]
-    in_bias = split[:, 1, :n_qkv].reshape(layers, 3, n_head)
+    grad_in = jnp.swapaxes(grad_in.reshape(layers, 3, n_head, width), 2, 3)
     return (
-        jnp.swapaxes(hidden_out, 0, 1),
-        jnp.swapaxes(grad_hidden, 0, 1),
-        jnp.swapaxes(grad_in, 2, 3).astype(F32),
-        jnp.stack([in_bias[:, 0], in_bias[:, 2]], axis=1),
-        grads[:, 2 * ff + n_qkv :].astype(F32),
-        grads[:, ff : 2 * ff].astype(F32),
-        split[:, 0, :ff],
-        grads[:, :ff].astype(F32),
-        shared[:, 0:2],
-        shared[:, 2:4],
-        shared[:, 4:6],
+        hidden_out,
+        grad_hidden,
+        grad_in.astype(F32),
+        grad_in_bias,
+        grad_out.astype(F32),
+        grad_up.astype(F32),
+        grad_up_bias,
+        grad_down.astype(F32),
+        grad_branch,
+        grad_gain,
+        grad_shift,
     )
 
 

time: 321 us -> 275 us (0.86)
  Pallas kernels: 282 us -> 259 us
  local copies, waits for them, and re-layouts: 24.1 us -> 4.65 us
  other arithmetic: 13.7 us -> 10.1 us
    pallas_call x1, Pallas kernels: 282 us -> 259 us  [local(): pl.pallas_call(functools.partial(kernel, n_dp, layers), out_shape=(jax.Sh...]
    slice x9 -> x0, local copies, waits for them, and re-layouts: 12.2 us -> none  [the longest x2 5.59 us: local(): grad_in = grads[:, 2 * ff:2 * ff + n_qkv].reshape(layers, 3, n_head, width)]
    convert_element_type x6 -> x4, other arithmetic: 11.4 us -> 10.1 us  [the longest x1 4.36 us: local(): grad_up.astype(F32)]
where the time goes in v2:
time: 275 us
  Pallas kernels  259 us (94%)
  other arithmetic  10.1 us (4%)
  local copies, waits for them, and re-layouts  4.65 us (2%)
    pallas_call x1, Pallas kernels, local(): pl.pallas_call(functools.partial(kernel, n_dp, layers), out_shape=(jax.Sh...  259 us

profile of v2, /device:TPU:0, one launch (start us, length us, event | category | flops | bytes accessed | tf_op | source)
XLA Modules:
  0.0 275.0 jit_solution(4314883431774800906)
XLA Ops:
  0.6 259.5 %shard_map.212 = (bf16[128,2,768]{2,1,0:T(2,128)(2,1)}, f32[128,2,768]{2,1,0:T(2,128)}, bf16[2,576,768]{2,1,0:T(8,128)(2,1)}, f32[2,2,192]{2,1,0:T(2,128)}, bf16...) custom-call(bf16[128,2,768]{2,1,0:T(2,128)(2,1)} %refs_0_.1, ...), custom_call_target="tpu_custom_call" | custom-call | tf_op jit(solution)/shard_map/pallas_call | solution.py:666
  260.1 0.0 copy-start
  260.2 4.4 %convert_element_type.22 = f32[2,768,768]{2,1,0:T(8,128)} convert(bf16[2,768,768]{2,1,0:T(8,128)(2,1)} %get-tuple-element.27) | non-fusion elementwise | flops 1179648 | bytes 7077888 | tf_op jit(solution)/shard_map/convert_element_type | solution.py:710
  264.5 0.0 copy-done
  264.5 0.0 copy-start.1
  264.5 2.5 convert_element_type.23
  267.1 0.0 copy-done.1
  267.1 0.0 copy-start.3
  267.1 0.0 copy-start.4
  267.1 2.1 convert_bitcast_fusion
  269.2 0.0 copy-start.2
  269.2 0.0 copy-start.9
  269.2 0.0 copy-start.8
  269.2 0.0 copy-start.7
  269.2 0.0 copy-start.6
  269.2 0.0 copy-start.5
  269.2 0.0 copy-done.3
  269.2 1.1 convert_element_type.21
  270.3 0.0 copy-done.4
  270.3 0.7 copy.31
  271.1 0.0 copy-done.2
  271.1 0.9 copy.32
  272.0 0.0 copy-done.9
  272.0 0.6 copy.33
  272.6 0.0 copy-done.8
  272.6 0.6 copy.34
  273.1 0.0 copy-done.7
  273.1 0.6 copy.35
  273.7 0.0 copy-done.6
  273.8 0.6 copy.36
  274.4 0.0 copy-done.5
  274.4 0.6 copy.37
Async XLA Ops:
  260.1 4.4 %copy-start = (bf16[2,768,768]{2,1,0:T(8,128)(2,1)S(1)}, bf16[2,768,768]{2,1,0:T(8,128)(2,1)}, u32[]{:S(2)}) copy-start(bf16[2,768,768]{2,1,0:T(8,128)(2,1)} %get-tuple-element.29) | copy-start | bytes 7077892
  264.5 2.6 copy-start.1
  267.1 2.1 copy-start.3
  267.1 3.2 %copy-start.4 = (bf16[128,2,768]{2,1,0:T(2,128)(2,1)S(1)}, bf16[128,2,768]{2,1,0:T(2,128)(2,1)}, u32[]{:S(2)}) copy-start(bf16[128,2,768]{2,1,0:T(2,128)(2,1)} %get-tuple-element.44) | copy-start | bytes 1179652
  269.2 1.9 copy-start.2
  269.2 2.8 %copy-start.9 = (f32[2,2,192]{2,1,0:T(2,128)S(1)}, f32[2,2,192]{2,1,0:T(2,128)}, u32[]{:S(2)}) copy-start(f32[2,2,192]{2,1,0:T(2,128)} %get-tuple-element.47) | copy-start | bytes 9220
  269.2 3.4 %copy-start.8 = (f32[2,768]{1,0:T(2,128)S(1)}, f32[2,768]{1,0:T(2,128)}, u32[]{:S(2)}) copy-start(f32[2,768]{1,0:T(2,128)} %get-tuple-element.50) | copy-start | bytes 18436
  269.2 4.0 %copy-start.7 = (f32[2,2,768]{2,1,0:T(2,128)S(1)}, f32[2,2,768]{2,1,0:T(2,128)}, u32[]{:S(2)}) copy-start(f32[2,2,768]{2,1,0:T(2,128)} %get-tuple-element.52) | copy-start | bytes 36868
  269.2 4.6 %copy-start.6 = (f32[2,2,768]{2,1,0:T(2,128)S(1)}, f32[2,2,768]{2,1,0:T(2,128)}, u32[]{:S(2)}) copy-start(f32[2,2,768]{2,1,0:T(2,128)} %get-tuple-element.53) | copy-start | bytes 36868
  269.2 5.1 %copy-start.5 = (f32[2,2,768]{2,1,0:T(2,128)S(1)}, f32[2,2,768]{2,1,0:T(2,128)}, u32[]{:S(2)}) copy-start(f32[2,2,768]{2,1,0:T(2,128)} %get-tuple-element.54) | copy-start | bytes 36868

commit v3 on v2

--- a/solution.py
+++ b/solution.py
@@ -40,18 +40,18 @@
         z = (dp // 2) % 4
         self.half = z // 2
         self.inner = (z == 1) | (z == 2)
+        self.inner_count = (z + 1) // 2 % 2
         self.edge = (z == 0) | (z == 3)
         self.x_dev = (dp + 1 - 2 * self.x, t)
         self.hop_dev = (dp + 2 * (1 - 2 * (z % 2)), t)
         self.mid_dev = (dp + 2 * (3 - 2 * z), t)
-        self.z2_dev = (dp + 2 * (2 - 4 * (z // 2)), t)
         self.outer_devs = []
         step = 8
         while step < n_dp:
             self.outer_devs.append((dp + step * (1 - 2 * ((dp // step) % 2)), t))
             step *= 2
-        self.vector_devs = [self.x_dev, self.hop_dev, self.z2_dev] + self.outer_devs
-        self.partners = [self.core, self.y, self.mid_dev] + self.vector_devs
+        self.partners = [self.core, self.y, self.x_dev, self.hop_dev]
+        self.inner_partners = [self.mid_dev] + self.outer_devs
 
 
 def remote(src, dst, send, recv, device):
@@ -62,8 +62,7 @@
 
 def kernel(n_dp, layers, *refs):
     (x_in, cot, lengths, padding, wt_h, in_bias, wo_h, wu_h, up_bias, wd_h, branch_bias, norm_gain, norm_shift,
-     hidden_out, grad_hidden, grad_in, grad_in_bias, grad_out, grad_up, grad_up_bias, grad_down,
-     grad_branch, grad_gain, grad_shift,
+     hidden_out, grad_hidden, grad_in, grad_out, grad_up, grad_down, small,
      WT, WO, WU, WD, XG, HG, G, DG, DF, DU, QKVT, PT, CT, DPT, DST, DCT, PART, RB, XRES, HRES, XH, RSTD, GR,
      RX0, RX1, RX2, RZ0, RZ1, RZ2, RXO, RZO, SX0, SX1, SZ0, SZ1, VB, RV, segc, segr, bcol, bup, vec,
      wsem, ag_s, ag_r, rs_s, rs_r, arx_s, arx_r, arz_s, arz_r, v_s, v_r, osem, credit_x, credit_z) = refs
@@ -86,7 +85,13 @@
     barrier = pltpu.get_barrier_semaphore()
     for device in net.partners:
         pl.semaphore_signal(barrier, inc=1, device_id=device, device_id_type=MESH)
-    pl.semaphore_wait(barrier, len(net.partners))
+
+    @pl.when(net.inner)
+    def _():
+        for device in net.inner_partners:
+            pl.semaphore_signal(barrier, inc=1, device_id=device, device_id_type=MESH)
+
+    pl.semaphore_wait(barrier, len(net.partners) + net.inner_count * len(net.inner_partners))
 
     def rows_at(r, t):
         return pl.ds(aligned(r * seq + t * block), block)
@@ -254,7 +259,7 @@
             at = slice(q * seq // 2, (q + 1) * seq // 2)
             PART[r, at] = dot(DPT[r, :, at], WT[l], TN).astype(BF)
 
-    per_layer = GR.shape[0] // layers
+    per_layer = 2 * ff + n_qkv + n_head
 
     def tokens_product(left, right, base):
         def strip(i, carry):
@@ -270,7 +275,7 @@
         at = pl.ds(aligned(base + n_qkv), n_head)
         GR[at] = sum(dot(CT[l, r], DG[l, r * seq : (r + 1) * seq], NN) for r in range(rows)).astype(BF)
 
-    units = GR.shape[0] // UNIT
+    units = layers * per_layer // UNIT
     part = UNIT // 2
     half = part // 2
     stages_x, stages_z = [], []
@@ -312,6 +317,12 @@
         src = src if staging is None else staging.at[u % SPACING]
         return remote(src, dst, which[1].at[u, s], which[2].at[u, s], device)
 
+    def last_of(which):
+        return units if which[0] is stages_x else units - 1
+
+    def live(which, u):
+        return (u >= 0) & (u <= last_of(which))
+
     def credit_of(which, s):
         return hops[s][1] if s in hops and hops[s][0] is which[0] else None
 
@@ -344,7 +355,7 @@
                 GR[at] = (GR[at].astype(F32) + landing[u % SLOTS].astype(F32)).astype(BF)
             if credit_of(which, s) is not None:
 
-                @pl.when(u < units - SLOTS)
+                @pl.when(u < last_of(which) + 1 - SLOTS)
                 def _():
                     pl.semaphore_signal(credit_of(which, s), inc=1, device_id=device, device_id_type=MESH)
 
@@ -374,7 +385,7 @@
         i, own = u // per_units, u % per_units
         for k, (end, _, _) in enumerate(sections):
 
-            @pl.when(own == end - 1)
+            @pl.when((own == end - 1) & (u < units))
             def _(k=k):
                 out_copy(i, k).start()
 
@@ -382,29 +393,22 @@
         t = now - lag
         for s in range(depth):
             u = t - SPACING * (s + 1)
-
-            @pl.when((u >= 0) & (u < units))
-            def _(s=s, u=u):
-                for which in both:
-                    stage_sent(which, s, u)
-
-        @pl.when((t >= 0) & (t < units))
-        def _():
             for which in both:
-                stage_send(which, 0, t)
-
+                pl.when(live(which, u))(functools.partial(stage_sent, which, s, u))
+        for which in both:
+            pl.when(live(which, t))(functools.partial(stage_send, which, 0, t))
         for s in range(depth):
             u = t - SPACING * (s + 1)
-
-            @pl.when((u >= 0) & (u < units))
-            def _(s=s, u=u):
-                for which in both:
+            for which in both:
+
+                @pl.when(live(which, u))
+                def _(which=which, s=s, u=u):
                     stage_recv(which, s, u)
                     if s + 1 < depth:
                         stage_send(which, s + 1, u)
-                if s + 1 == depth:
-                    unit_done(u)
-
+
+        u = t - SPACING * depth
+        pl.when((u >= 0) & (u < units))(functools.partial(unit_done, u))
         return carry
 
     for r in range(rows):
@@ -530,31 +534,20 @@
     lax.fori_loop(0, layers, backward, 0)
 
     def vector_copy(k):
-        if k < 2:
-            return remote(VB.at[0], RV.at[k, 0], v_s.at[k], v_r.at[k], (net.core, net.y)[k])
-        return remote(VB, RV.at[k], v_s.at[k], v_r.at[k], net.vector_devs[k - 2])
-
-    n_vector = 2 + len(net.vector_devs)
-    now, last = layers * per_units, lag + units + SPACING * depth
-    for k in range(n_vector + 1):
-        if k > 0:
-            vector_copy(k - 1).wait()
-            if k - 1 < 2:
-                VB[0] += RV[k - 1, 0]
-            else:
-                VB[...] += RV[k - 1]
-        if k < n_vector:
-            vector_copy(k).start()
-        lax.fori_loop(now, now + 2, tick, 0)
-        now += 2
-    lax.fori_loop(now, last, tick, 0)
-    for l in range(layers):
-        grad_branch[l] = VB[0, l, 0:2]
-        grad_gain[l] = VB[0, l, 2:4]
-        grad_shift[l] = VB[0, l, 4:6]
-        grad_up_bias[l : l + 1] = VB[1, l, 0:1, :ff]
-        for c, at in ((0, 0), (1, 2 * n_head)):
-            grad_in_bias[l, c : c + 1] = VB[1, l, 1:2, at : at + n_head]
+        return remote(VB.at[0], RV.at[k], v_s.at[k], v_r.at[k], (net.core, net.y)[k])
+
+    now = layers * per_units
+    for k in range(2):
+        vector_copy(k).start()
+        lax.fori_loop(now, now + min(1, lag // 2), tick, 0)
+        now += min(1, lag // 2)
+        vector_copy(k).wait()
+        VB[0] += RV[k]
+    base = layers * per_layer
+    GR[base : base + UNIT] = jnp.zeros((UNIT, width), BF)
+    GR[base : base + 16 * layers] = VB[...].reshape(16 * layers, width).astype(BF)
+    lax.fori_loop(now, lag + units + 1 + SPACING * depth, tick, 0)
+    small[...] = GR[base : base + 16 * layers].astype(F32)
     for i in range(layers):
         for k in range(len(sections)):
             out_copy(i, k).wait()
@@ -588,7 +581,6 @@
     while 8 << outer < n_dp:
         outer += 1
     depth = 5 + outer
-    n_vector = 5 + outer
     vmem = pltpu.VMEM
     dma = pltpu.SemaphoreType.DMA
     scratch = [
@@ -614,7 +606,7 @@
         vmem((rows, block, width), F32),
         vmem((layers, 2, rows, block, width), BF),
         vmem((layers, 2, rows, block, 1), F32),
-        vmem((layers * per_layer, width), BF),
+        vmem((layers * per_layer + UNIT, width), BF),
         vmem((SLOTS, part // 2, width), BF),
         vmem((SLOTS, part // 2, width), BF),
         vmem((SLOTS, part // 2, width), BF),
@@ -628,7 +620,7 @@
         vmem((SPACING, part, width), BF),
         vmem((SPACING, part // 2, width), BF),
         vmem((2, layers, 8, width), F32),
-        vmem((n_vector, 2, layers, 8, width), F32),
+        vmem((2, layers, 8, width), F32),
         vmem((rows, seq, 1), jnp.int32),
         vmem((rows, 1, seq), jnp.int32),
         vmem((layers, n_qkv, 1), F32),
@@ -639,48 +631,32 @@
         dma((rows, 3)),
         dma((rows, 3)),
         dma((rows, 3)),
-        dma((layers * per_layer // UNIT, depth)),
-        dma((layers * per_layer // UNIT, depth)),
-        dma((layers * per_layer // UNIT, depth)),
-        dma((layers * per_layer // UNIT, depth)),
-        dma((n_vector,)),
-        dma((n_vector,)),
+        dma((layers * per_layer // UNIT + 1, depth)),
+        dma((layers * per_layer // UNIT + 1, depth)),
+        dma((layers * per_layer // UNIT + 1, depth)),
+        dma((layers * per_layer // UNIT + 1, depth)),
+        dma((2,)),
+        dma((2,)),
         dma((layers, 4)),
         pltpu.SemaphoreType.REGULAR,
         pltpu.SemaphoreType.REGULAR,
     ]
     whole, anywhere = pl.BlockSpec(memory_space=vmem), pl.BlockSpec(memory_space=pl.ANY)
     scalars = pl.BlockSpec(memory_space=pltpu.SMEM)
-    (
-        hidden_out,
-        grad_hidden,
-        grad_in,
-        grad_in_bias,
-        grad_out,
-        grad_up,
-        grad_up_bias,
-        grad_down,
-        grad_branch,
-        grad_gain,
-        grad_shift,
-    ) = pl.pallas_call(
+    results = pl.pallas_call(
         functools.partial(kernel, n_dp, layers),
         out_shape=(
             jax.ShapeDtypeStruct(hidden_in.shape, BF),
             jax.ShapeDtypeStruct(hidden_in.shape, F32),
             jax.ShapeDtypeStruct((layers, n_qkv, width), BF),
-            jax.ShapeDtypeStruct(input_bias.shape, F32),
             jax.ShapeDtypeStruct(output_weight.shape, BF),
             jax.ShapeDtypeStruct(up_weight.shape, BF),
-            jax.ShapeDtypeStruct(up_bias.shape, F32),
             jax.ShapeDtypeStruct(down_weight.shape, BF),
-            jax.ShapeDtypeStruct(branch_bias.shape, F32),
-            jax.ShapeDtypeStruct(norm_gain.shape, F32),
-            jax.ShapeDtypeStruct(norm_shift.shape, F32),
+            jax.ShapeDtypeStruct((16 * layers, width), F32),
         ),
         in_specs=[whole, whole, scalars, scalars, anywhere, whole, anywhere, anywhere, whole, anywhere]
         + [whole] * 3,
-        out_specs=(whole, whole, anywhere, whole, anywhere, anywhere, whole, anywhere, whole, whole, whole),
+        out_specs=(whole, whole, anywhere, anywhere, anywhere, anywhere, whole),
         scratch_shapes=scratch,
         compiler_params=pltpu.CompilerParams(
             collective_id=0, has_side_effects=True, vmem_limit_bytes=63 << 20
@@ -700,20 +676,65 @@
         norm_gain,
         norm_shift,
     )
+    pieces = 4
+
+    def strip(array):
+        return pl.BlockSpec((1, array.shape[1] // pieces, width), lambda l, c: (l, c, 0))
+
+    strips = [strip(array) for array in results[2:6]]
+    fixed = [
+        jax.ShapeDtypeStruct(shape, F32)
+        for shape in (input_bias.shape, up_bias.shape, branch_bias.shape, norm_gain.shape, norm_shift.shape)
+    ]
+    hidden_out, grad_hidden, grad_in, grad_out, grad_up, grad_down, *vectors = pl.pallas_call(
+        functools.partial(finish, layers, pieces),
+        grid=(layers, pieces),
+        out_shape=[jax.ShapeDtypeStruct(array.shape, array.dtype) for array in results[:2]]
+        + [jax.ShapeDtypeStruct(array.shape, F32) for array in results[2:6]]
+        + fixed,
+        in_specs=[whole] * 2 + strips + [whole],
+        out_specs=[whole] * 2 + strips + [whole] * 5,
+    )(*results)
+    grad_in_bias, grad_up_bias, grad_branch, grad_gain, grad_shift = vectors
     grad_in = jnp.swapaxes(grad_in.reshape(layers, 3, n_head, width), 2, 3)
     return (
         hidden_out,
         grad_hidden,
-        grad_in.astype(F32),
+        grad_in,
         grad_in_bias,
-        grad_out.astype(F32),
-        grad_up.astype(F32),
+        grad_out,
+        grad_up,
         grad_up_bias,
-        grad_down.astype(F32),
+        grad_down,
         grad_branch,
         grad_gain,
         grad_shift,
     )
+
+
+def finish(layers, pieces, *refs):
+    hidden, grad_hidden, *grads = refs[:6]
+    small = refs[6]
+    hidden_out, grad_hidden_out, *outs = refs[7:13]
+    grad_in_bias, grad_up_bias, grad_branch, grad_gain, grad_shift = refs[13:18]
+    step = pl.program_id(0) * pieces + pl.program_id(1)
+
+    @pl.when(step == 0)
+    def _():
+        hidden_out[...] = hidden[...]
+        grad_hidden_out[...] = grad_hidden[...]
+        n_head, ff = grad_in_bias.shape[2], grad_up_bias.shape[1]
+        for l in range(layers):
+            shared, split = 8 * l, 8 * (layers + l)
+            grad_branch[l] = small[shared : shared + 2]
+            grad_gain[l] = small[shared + 2 : shared + 4]
+            grad_shift[l] = small[shared + 4 : shared + 6]
+            grad_up_bias[l : l + 1] = small[split : split + 1, :ff]
+            for c in range(2):
+                grad_in_bias[l, c : c + 1] = small[split + 1 : split + 2, 2 * c * n_head : (2 * c + 1) * n_head]
+
+    for grad, out in zip(grads, outs, strict=True):
+        out[...] = grad[...].astype(F32)
 
 
 def solution(mesh):

time: 275 us -> 267 us (0.971)
  other arithmetic: 10.1 us -> 0 us
  Pallas kernels: 259 us -> 266 us
  local copies, waits for them, and re-layouts: 4.65 us -> 0 us
    pallas_call x0 -> x1, Pallas kernels: none -> 10.3 us  [local(): pl.pallas_call(functools.partial(finish, layers, pieces), grid=(layers, p...]
    convert_element_type x4 -> x0, other arithmetic: 10.1 us -> none  [the longest x1 4.36 us: local(): grad_up.astype(F32)]
    unnamed x27 -> x0, local copies, waits for them, and re-layouts: 4.65 us -> none
    pallas_call x1, Pallas kernels: 259 us -> 256 us  [local(): pl.pallas_call(functools.partial(kernel, n_dp, layers), out_shape=(jax.Sh...]
where the time goes in v3:
time: 267 us
  Pallas kernels  266 us (100%)
    pallas_call x1, Pallas kernels, local(): pl.pallas_call(functools.partial(kernel, n_dp, layers), out_shape=(jax.Sh...  256 us
    pallas_call x1, Pallas kernels, local(): pl.pallas_call(functools.partial(finish, layers, pieces), grid=(layers, p...  10.3 us

profile of v3, /device:TPU:0, one launch (start us, length us, event | category | flops | bytes accessed | tf_op | source)
XLA Modules:
  0.0 267.0 jit_solution(6431621600391922802)
XLA Ops:
  0.6 255.9 %shard_map.212 = (bf16[128,2,768]{2,1,0:T(2,128)(2,1)}, f32[128,2,768]{2,1,0:T(2,128)}, bf16[2,576,768]{2,1,0:T(8,128)(2,1)}, bf16[2,192,768]{2,1,0:T(8,128)(2,1...) custom-call(bf16[128,2,768]{2,1,0:T(2,128)(2,1)} %refs_0_.1, ...), custom_call_target="tpu_custom_call" | custom-call | tf_op jit(solution)/shard_map/pallas_call | solution.py:646
  256.5 10.3 %shard_map.213 = (bf16[128,2,768]{2,1,0:T(2,128)(2,1)}, f32[128,2,768]{2,1,0:T(2,128)}, f32[2,576,768]{2,1,0:T(8,128)}, f32[2,192,768]{2,1,0:T(8,128)}, f32[2,76...) custom-call(bf16[128,2,768]{2,1,0:T(2,128)(2,1)} %get-tuple-element., ...), custom_call_target="tpu_custom_call" | custom-call | tf_op jit(solution)/shard_map/pallas_call | solution.py:689
